TPU v7x, 256 devices: a whole 4x4x8 slice. The times are simulated.
256 devices in a mesh: ctx: 64 (over z, x, core), kv: 4 (over y).
Axes of the slice: x: 4, y: 4, z: 8, core: 2. Of those that a mesh axis runs over, the one named last changes fastest.
Arguments:
- queries: bfloat16 [32768, 4096], P(('ctx', 'kv')), may hold values from -162 to 162
- keys: bfloat16 [32768, 512], P(('ctx', 'kv')), may hold values from -6 to 6
- values: bfloat16 [32768, 512], P(('ctx', 'kv')), may hold values from -6 to 6
- grad_out: bfloat16 [32768, 4096], P(('ctx', 'kv')), may hold values from -6 to 6
- doc_lengths: int32 [64], replicated, may hold values from 1 to 1024, 32768 in all
Outputs:
- query_grad: bfloat16 [32768, 4096], P(('ctx', 'kv'))
- key_grad: bfloat16 [32768, 512], P(('ctx', 'kv'))
- value_grad: bfloat16 [32768, 512], P(('ctx', 'kv'))
Inputs may be any that keep to these rules, and one draw needn't show every extreme that they name: `doc_lengths`: 64 document lengths in sequence order; they sum to 32768 and the longest is exactly 1024.
All inputs are finite; a program needn't handle non-finite values.
Results may differ from a plain program's by a relative error of at most 0.0055.
Values may be sent and summed in bfloat16 or wider, within the bound.
No kernel may reach another device: no remote copies, remote signals or barrier semaphores. Data moves between devices by JAX's collectives and lax.ppermute only.
A program may use at most 128 MiB of HBM per device.

v0:
```python
import math

import jax
import jax.numpy as jnp
from jax import lax
from jax.experimental import pallas as pl
from jax.experimental.pallas import tpu as pltpu
from jax.sharding import PartitionSpec as P

HD = 128
AXES = ("ctx", "kv")
BACK = 8
SLOTS = 12
NEG = -1e30
NT = (((1,), (1,)), ((), ()))
TN = (((0,), (0,)), ((), ()))
SCALE = 1.0 / math.sqrt(HD)
SCALE_LOG2 = math.log2(math.e) / math.sqrt(HD)


def device_of(n_ctx, group, half, part):
    if group < n_ctx // 2:
        return (2 * group + half) * 4 + part
    return (n_ctx - 1 - (2 * (group - n_ctx // 2) + half)) * 4 + part + 2


def pairs(n_ctx, move):
    found = []
    for group in range(n_ctx):
        for half in range(2):
            for part in range(2):
                target = move(group, half, part)
                if 0 <= target[0] < n_ctx:
                    found.append((device_of(n_ctx, group, half, part), device_of(n_ctx, *target)))
    return found


def place():
    n_ctx = lax.axis_size("ctx")
    slot = lax.axis_index("ctx")
    lane = lax.axis_index("kv")
    upper = lane // 2
    block = jnp.where(upper == 0, slot, 2 * n_ctx - 1 - slot)
    return block // 2, block % 2, lane % 2


def kernel(
    lengths_ref, q_ref, g_ref, x_ref, y_refs, dq_ref, keep_ref, send_ref,
    win, acc, s_scr, dp_scr, p_scr, ds_scr, lo_scr, in_sem, out_sem,
):
    step = pl.program_id(0)
    rows = q_ref.shape[0]
    heads = q_ref.shape[1] // HD
    width = (BACK + 1) * rows
    kv_width = win.shape[1] // 2
    group, half, part = place()
    first = 2 * half + part
    sources = (x_ref,) + tuple(y_refs)

    def spot(which, h_rel, y_rel):
        return pl.ds(pl.multiple_of((4 * which + 2 * (half ^ h_rel) + (part ^ y_rel)) * rows, rows), rows)

    def arrivals():
        copies = []
        n = 0
        for which in (2, 1, 0):
            for h_rel in range(2):
                for y_rel in range(2):
                    copies.append(
                        pltpu.make_async_copy(sources[n], win.at[spot(which, h_rel, y_rel)], in_sem.at[n])
                    )
                    n += 1
        return copies

    @pl.when(step == 0)
    def _():
        for copy in arrivals():
            copy.start()
        acc[...] = jnp.zeros_like(acc)
        lens = lengths_ref[...].astype(jnp.float32)
        docs = lens.shape[1]
        below = lax.broadcasted_iota(jnp.int32, (docs, docs), 1) <= lax.broadcasted_iota(
            jnp.int32, (docs, docs), 0
        )
        ends = jnp.sum(jnp.where(below, lens, 0.0), axis=1, keepdims=True)
        start = (4 * group + first) * rows
        pos = (start + lax.broadcasted_iota(jnp.int32, (1, rows), 1)).astype(jnp.float32)
        low = jnp.max(jnp.where(ends <= pos, ends, 0.0), axis=0, keepdims=True).astype(jnp.int32)
        lo_scr[...] = jnp.broadcast_to(low - (start - BACK * rows), lo_scr.shape)
        for copy in arrivals():
            copy.wait()

    lo = lo_scr[0:1, :]
    lo2 = jnp.concatenate([lo, lo], axis=1)
    window = pl.ds(pl.multiple_of(first * rows, rows), width)
    k_cols = pl.ds(pl.multiple_of(step * HD, HD), HD)
    v_cols = pl.ds(pl.multiple_of(kv_width + step * HD, HD), HD)
    keys = win[window, k_cols]
    values = win[window, v_cols]
    column = lax.broadcasted_iota(jnp.int32, (1, 2 * rows), 1) % rows

    def head(ref, index):
        return ref[:, index * HD : (index + 1) * HD]

    for hp in range(heads // 2):
        lanes = slice(hp * 2 * rows, (hp + 1) * 2 * rows)
        q2 = jnp.concatenate([head(q_ref, 2 * hp), head(q_ref, 2 * hp + 1)], axis=0)
        g2 = jnp.concatenate([head(g_ref, 2 * hp), head(g_ref, 2 * hp + 1)], axis=0)
        s_scr[hp] = lax.dot_general(keys, q2, NT, preferred_element_type=jnp.float32)
        dp_scr[hp] = lax.dot_general(values, g2, NT, preferred_element_type=jnp.float32)
        top = jnp.full((8, 2 * rows), NEG, jnp.float32)
        for t in range(BACK + 1):
            here = slice(t * rows, (t + 1) * rows)
            tile = s_scr[hp, here, :]
            key_row = lax.broadcasted_iota(jnp.int32, (rows, 2 * rows), 0) + t * rows
            allowed = key_row >= lo2
            if t == BACK:
                allowed = allowed & (key_row - BACK * rows <= column)
            tile = jnp.where(allowed, tile, NEG)
            s_scr[hp, here, :] = tile
            top = jnp.maximum(top, jnp.max(tile.reshape(rows // 8, 8, 2 * rows), axis=0))
        top = jnp.max(top, axis=0, keepdims=True) * SCALE_LOG2
        total = jnp.zeros((8, 2 * rows), jnp.float32)
        dots = jnp.zeros((8, 2 * rows), jnp.float32)
        for t in range(BACK + 1):
            here = slice(t * rows, (t + 1) * rows)
            weight = jnp.exp2(s_scr[hp, here, :] * SCALE_LOG2 - top)
            s_scr[hp, here, :] = weight
            total = total + jnp.sum(weight.reshape(rows // 8, 8, 2 * rows), axis=0)
            dots = dots + jnp.sum((weight * dp_scr[hp, here, :]).reshape(rows // 8, 8, 2 * rows), axis=0)
        inverse = 1.0 / jnp.sum(total, axis=0, keepdims=True)
        delta = jnp.sum(dots, axis=0, keepdims=True) * inverse
        for t in range(BACK + 1):
            here = slice(t * rows, (t + 1) * rows)
            prob = s_scr[hp, here, :] * inverse
            p_scr[here, lanes] = prob.astype(jnp.bfloat16)
            ds_scr[here, lanes] = (prob * (dp_scr[hp, here, :] - delta)).astype(jnp.bfloat16)
        dq = lax.dot_general(ds_scr[:, lanes], keys, TN, preferred_element_type=jnp.float32) * SCALE
        dq = dq.astype(jnp.bfloat16)
        dq_ref[:, 2 * hp * HD : (2 * hp + 1) * HD] = dq[:rows]
        dq_ref[:, (2 * hp + 1) * HD : (2 * hp + 2) * HD] = dq[rows:]
    q_all = jnp.concatenate([head(q_ref, index) for index in range(heads)], axis=0)
    g_all = jnp.concatenate([head(g_ref, index) for index in range(heads)], axis=0)
    acc[window, v_cols] = jnp.dot(p_scr[...], g_all, preferred_element_type=jnp.float32).astype(jnp.bfloat16)
    acc[window, k_cols] = (jnp.dot(ds_scr[...], q_all, preferred_element_type=jnp.float32) * SCALE).astype(
        jnp.bfloat16
    )

    @pl.when(step == pl.num_programs(0) - 1)
    def _():
        copies = []
        n = 0
        for which in range(3):
            for y_rel in range(2):
                for h_rel, out in ((1, send_ref), (0, keep_ref)):
                    copies.append(
                        pltpu.make_async_copy(
                            acc.at[spot(which, h_rel, y_rel)], out.at[which, y_rel], out_sem.at[n]
                        )
                    )
                    n += 1
        for copy in copies:
            copy.start()
        for copy in copies:
            copy.wait()


def attention(lengths, queries, grad_out, own, arrived):
    rows, q_width = queries.shape
    kv_width = own.shape[1] // 2
    kv_heads = kv_width // HD
    span = q_width // kv_heads
    width = (BACK + 1) * rows
    heads = span // HD
    by_head = pl.BlockSpec((rows, span), lambda i: (0, i))
    anywhere = pl.BlockSpec(memory_space=pl.ANY)
    part = jax.ShapeDtypeStruct((3, 2, rows, 2 * kv_width), jnp.bfloat16)
    return pl.pallas_call(
        kernel,
        grid=(kv_heads,),
        in_specs=[
            pl.BlockSpec(lengths.shape, lambda i: (0, 0)),
            by_head,
            by_head,
            anywhere,
            tuple([anywhere] * len(arrived)),
        ],
        out_specs=[by_head, anywhere, anywhere],
        out_shape=[jax.ShapeDtypeStruct((rows, q_width), jnp.bfloat16), part, part],
        scratch_shapes=[
            pltpu.VMEM((SLOTS * rows, 2 * kv_width), jnp.bfloat16),
            pltpu.VMEM((SLOTS * rows, 2 * kv_width), jnp.bfloat16),
            pltpu.VMEM((heads // 2, width, 2 * rows), jnp.float32),
            pltpu.VMEM((heads // 2, width, 2 * rows), jnp.float32),
            pltpu.VMEM((width, heads * rows), jnp.bfloat16),
            pltpu.VMEM((width, heads * rows), jnp.bfloat16),
            pltpu.VMEM((8, rows), jnp.int32),
            pltpu.SemaphoreType.DMA((SLOTS,)),
            pltpu.SemaphoreType.DMA((SLOTS,)),
        ],
        compiler_params=pltpu.CompilerParams(vmem_limit_bytes=56 * 2**20),
    )(lengths, queries, grad_out, own, tuple(arrived))


def body(queries, keys, values, grad_out, doc_lengths):
    n_ctx = lax.axis_size("ctx")
    swap_part = pairs(n_ctx, lambda g, h, y: (g, h, 1 - y))
    swap_half = pairs(n_ctx, lambda g, h, y: (g, 1 - h, y))

    def ahead(steps):
        return pairs(n_ctx, lambda g, h, y: (g + steps, h, y))

    def sent(value, plan):
        return lax.ppermute(value, AXES, plan)

    def added(*terms):
        return sum(term.astype(jnp.float32) for term in terms)

    own = jnp.concatenate([keys, values], axis=1)
    gathered = []
    for steps in range(3):
        mine = own if steps == 0 else sent(own, ahead(steps))
        other = sent(mine, swap_part)
        gathered += [mine, other, sent(mine, swap_half), sent(other, swap_half)]
    query_grad, keep, send = attention(
        doc_lengths.reshape(1, -1), queries, grad_out, own, gathered[1:]
    )
    got = sent(send, swap_half)
    total = None
    for which in range(3):
        both = added(keep[which], got[which]).astype(jnp.bfloat16)
        summed = added(both[0], sent(both[1], swap_part))
        if which < 2:
            summed = sent(summed.astype(jnp.bfloat16), ahead(which - 2)).astype(jnp.float32)
        total = summed if total is None else total + summed
    total = total.astype(jnp.bfloat16)
    kv_width = keys.shape[1]
    return query_grad, total[:, :kv_width], total[:, kv_width:]


def solution(mesh):
    rows = P(AXES, None)
    return jax.shard_map(
        body,
        mesh=mesh,
        in_specs=(rows, rows, rows, rows, P()),
        out_specs=(rows, rows, rows),
        check_vma=False,
    )
```

profile of v0, /device:TPU:230, one launch (start us, length us, event | category | flops | bytes accessed | tf_op | source)
XLA Modules:
  0.0 103.4 jit_solution(17027501699348122280)
XLA Ops:
  0.6 0.9 constant_dynamic-update-slice_fusion.1
  1.5 0.9 constant_dynamic-update-slice_fusion.x_ref
  2.5 0.0 copy-start
  2.5 4.8 %collective-permute-start.7 = (bf16[128,1024]{1,0:T(8,128)(2,1)S(1)}, bf16[128,1024]{1,0:T(8,128)(2,1)S(1)}, u32[]{:S(2)}, u32[]{:S(2)}) collective-permute-start(bf16[128,1024]{1,0:T(8,128)(2,1)S(1)} %constant_dynamic-update-slice_fusion.x_ref), channel_id=1, source_target_pairs={{0,16},{1,17},{4,20},{5,21},{8,24},{9,25},{12,28},{13,29},{16,32},... | collective-permute-start | bytes 786440 | tf_op jit(solution)/shard_map/ppermute | solution.py:214
  7.3 2.8 %collective-permute-start.3 = (bf16[128,1024]{1,0:T(8,128)(2,1)S(1)}, bf16[128,1024]{1,0:T(8,128)(2,1)S(1)}, u32[]{:S(2)}, u32[]{:S(2)}) collective-permute-start(bf16[128,1024]{1,0:T(8,128)(2,1)S(1)} %constant_dynamic-update-slice_fusion.x_ref), channel_id=1, source_target_pairs={{0,8},{1,9},{4,12},{5,13},{8,16},{9,17},{12,20},{13,21},{16,24},{1... | collective-permute-start | bytes 786440 | tf_op jit(solution)/shard_map/ppermute | solution.py:214
  10.1 1.0 %collective-permute-start.1 = (bf16[128,1024]{1,0:T(8,128)(2,1)S(1)}, bf16[128,1024]{1,0:T(8,128)(2,1)S(1)}, u32[]{:S(2)}, u32[]{:S(2)}) collective-permute-start(bf16[128,1024]{1,0:T(8,128)(2,1)S(1)} %constant_dynamic-update-slice_fusion.x_ref), channel_id=1, source_target_pairs={{0,4},{1,5},{4,0},{5,1},{8,12},{9,13},{12,8},{13,9},{16,20},{17,21... | collective-permute-start | bytes 786440 | tf_op jit(solution)/shard_map/ppermute | solution.py:214
  11.1 0.7 collective-permute-start
  11.8 6.1 %collective-permute-done.7.y_refs_7_ = bf16[128,1024]{1,0:T(8,128)(2,1)S(1)} collective-permute-done((bf16[128,1024]{1,0:T(8,128)(2,1)S(1)}, bf16[128,1024]{1,0:T(8,128)(2,1)S(1)}, u32[]{:S(2)}, u32[]{:S(2)}) %collective-permute-start.7) | collective-permute-done | bytes 262176 | tf_op jit(solution)/shard_map/ppermute | solution.py:214
  17.9 0.0 copy-start.1
  17.9 1.6 %collective-permute-start.8 = (bf16[128,1024]{1,0:T(8,128)(2,1)S(1)}, bf16[128,1024]{1,0:T(8,128)(2,1)S(1)}, u32[]{:S(2)}, u32[]{:S(2)}) collective-permute-start(bf16[128,1024]{1,0:T(8,128)(2,1)S(1)} %collective-permute-done.7.y_refs_7_), channel_id=1, source_target_pairs={{0,1},{1,0},{4,5},{5,4},{8,9},{9,8},{12,13},{13,12},{16,17},{17,16... | collective-permute-start | bytes 786440 | tf_op jit(solution)/shard_map/ppermute | solution.py:214
  19.5 4.4 %collective-permute-done.3.y_refs_3_ = bf16[128,1024]{1,0:T(8,128)(2,1)S(1)} collective-permute-done((bf16[128,1024]{1,0:T(8,128)(2,1)S(1)}, bf16[128,1024]{1,0:T(8,128)(2,1)S(1)}, u32[]{:S(2)}, u32[]{:S(2)}) %collective-permute-start.3) | collective-permute-done | bytes 262176 | tf_op jit(solution)/shard_map/ppermute | solution.py:214
  23.9 1.6 %collective-permute-start.4 = (bf16[128,1024]{1,0:T(8,128)(2,1)S(1)}, bf16[128,1024]{1,0:T(8,128)(2,1)S(1)}, u32[]{:S(2)}, u32[]{:S(2)}) collective-permute-start(bf16[128,1024]{1,0:T(8,128)(2,1)S(1)} %collective-permute-done.3.y_refs_3_), channel_id=1, source_target_pairs={{0,1},{1,0},{4,5},{5,4},{8,9},{9,8},{12,13},{13,12},{16,17},{17,16... | collective-permute-start | bytes 786440 | tf_op jit(solution)/shard_map/ppermute | solution.py:214
  25.5 0.0 collective-permute-start.9
  25.5 0.0 collective-permute-done.1.y_refs_1_
  25.5 0.0 copy-start.3
  25.5 0.5 collective-permute-start.5
  26.0 2.7 %collective-permute-done.y_refs_0_ = bf16[128,1024]{1,0:T(8,128)(2,1)S(1)} collective-permute-done((bf16[128,1024]{1,0:T(8,128)(2,1)S(1)}, bf16[128,1024]{1,0:T(8,128)(2,1)S(1)}, u32[]{:S(2)}, u32[]{:S(2)}) %collective-permute-start) | collective-permute-done | bytes 262176 | tf_op jit(solution)/shard_map/ppermute | solution.py:214
  28.7 0.0 copy-start.4
  28.7 0.6 collective-permute-start.2
  29.4 5.0 %collective-permute-done.8.y_refs_8_ = bf16[128,1024]{1,0:T(8,128)(2,1)S(1)} collective-permute-done((bf16[128,1024]{1,0:T(8,128)(2,1)S(1)}, bf16[128,1024]{1,0:T(8,128)(2,1)S(1)}, u32[]{:S(2)}, u32[]{:S(2)}) %collective-permute-start.8) | collective-permute-done | bytes 262176 | tf_op jit(solution)/shard_map/ppermute | solution.py:214
  34.4 0.0 copy-start.5
  34.4 0.6 collective-permute-start.10
  35.0 5.0 %collective-permute-done.4.y_refs_4_ = bf16[128,1024]{1,0:T(8,128)(2,1)S(1)} collective-permute-done((bf16[128,1024]{1,0:T(8,128)(2,1)S(1)}, bf16[128,1024]{1,0:T(8,128)(2,1)S(1)}, u32[]{:S(2)}, u32[]{:S(2)}) %collective-permute-start.4) | collective-permute-done | bytes 262176 | tf_op jit(solution)/shard_map/ppermute | solution.py:214
  40.0 0.0 copy-start.6
  40.0 0.1 collective-permute-start.6
  40.1 0.0 collective-permute-done.9.y_refs_9_
  40.1 0.0 collective-permute-done.5.y_refs_5_
  40.1 0.0 copy-start.8
  40.1 0.0 collective-permute-done.2.y_refs_2_
  40.1 0.0 copy-start.9
  40.1 0.0 collective-permute-done.10.y_refs_10_
  40.2 0.0 copy-start.10
  40.2 1.4 %collective-permute-done.6.y_refs_6_ = bf16[128,1024]{1,0:T(8,128)(2,1)S(1)} collective-permute-done((bf16[128,1024]{1,0:T(8,128)(2,1)S(1)}, bf16[128,1024]{1,0:T(8,128)(2,1)S(1)}, u32[]{:S(2)}, u32[]{:S(2)}) %collective-permute-start.6) | collective-permute-done | bytes 262176 | tf_op jit(solution)/shard_map/ppermute | solution.py:214
  41.5 0.0 copy-start.11
  41.5 0.0 copy-done
  41.5 0.0 copy-done.1
  41.5 0.0 copy-done.2
  41.5 0.0 copy-done.3
  41.5 0.0 copy-done.4
  41.6 0.0 copy-done.5
  41.6 0.0 copy-done.6
  41.6 0.0 copy-done.7
  41.6 0.0 copy-done.8
  41.6 0.0 copy-done.9
  41.6 0.0 copy-done.10
  41.6 0.6 copy-done.11
  42.2 27.8 %shard_map.76 = (bf16[128,4096]{1,0:T(8,128)(2,1)}, bf16[3,2,128,1024]{3,2,1,0:T(8,128)(2,1)}, bf16[3,2,128,1024]{3,2,1,0:T(8,128)(2,1)}) custom-call(s32[1,64]{1,0:T(1,128)} %bitcast.22, bf16[128,4096]{1,0:T(8,128)(2,1)} %q_ref.1, bf16[128,4096]{1,0:T(8,128)(2,1)} %g_ref.1, bf16[128,1024]{1,0:T(8,128)(2,1)} %copy-done, bf16[128,1024]{1,0:T(8,128)(2,1)} %copy-done.4, ...), custom_call_target="tpu_custom_call" | custom-call | tf_op jit(solution)/shard_map/pallas_call | solution.py:178
  70.0 0.4 collective-permute-start.11
  70.4 3.5 %collective-permute-done.11 = bf16[3,2,128,1024]{3,2,1,0:T(8,128)(2,1)S(1)} collective-permute-done((bf16[3,2,128,1024]{3,2,1,0:T(8,128)(2,1)}, bf16[3,2,128,1024]{3,2,1,0:T(8,128)(2,1)S(1)}, u32[]{:S(2)}, u32[]{:S(2)}) %collective-permute-start.11) | collective-permute-done | bytes 1572896 | tf_op jit(solution)/shard_map/ppermute | solution.py:214
  73.9 2.0 %add_convert_fusion.2 = (bf16[1,2,128,1024]{3,2,1,0:T(8,128)(2,1)S(1)}, bf16[1,2,128,1024]{3,2,1,0:T(8,128)(2,1)S(1)}, bf16[1,2,128,1024]{3,2,1,0:T(8,128)(2,1)S(1)}) fusion(bf16[3,2,128,1024]{3,2,1,0:T(8,128)(2,1)S(1)} %collective-permute-done.11, bf16[3,2,128,1024]{3,2,1,0:T(8,128)(2,1)} %get-tuple-element.7), kind=kLoop, calls=%fused_computation.2 | loop fusion | flops 3145728 | bytes 4718592 | tf_op jit(solution)/shard_map/convert_element_type | solution.py:231
  76.0 1.4 %collective-permute-start.14 = (bf16[128,1024]{1,0:T(8,128)(2,1)S(1)}, bf16[128,1024]{1,0:T(8,128)(2,1)S(1)}, u32[]{:S(2)}, u32[]{:S(2)}) collective-permute-start(bf16[128,1024]{1,0:T(8,128)(2,1)S(1)} %slice_bitcast_fusion.2), channel_id=1, source_target_pairs={{0,1},{1,0},{4,5},{5,4},{8,9},{9,8},{12,13},{13,12},{16,17},{17,16... | collective-permute-start | bytes 786440 | tf_op jit(solution)/shard_map/ppermute | solution.py:214
  77.4 0.8 collective-permute-start.12
  78.2 1.4 %collective-permute-start.16 = (bf16[128,1024]{1,0:T(8,128)(2,1)S(1)}, bf16[128,1024]{1,0:T(8,128)(2,1)S(1)}, u32[]{:S(2)}, u32[]{:S(2)}) collective-permute-start(bf16[128,1024]{1,0:T(8,128)(2,1)S(1)} %slice_bitcast_fusion), channel_id=1, source_target_pairs={{0,1},{1,0},{4,5},{5,4},{8,9},{9,8},{12,13},{13,12},{16,17},{17,16... | collective-permute-start | bytes 786440 | tf_op jit(solution)/shard_map/ppermute | solution.py:214
  79.7 5.5 %collective-permute-done.14 = bf16[128,1024]{1,0:T(8,128)(2,1)S(1)} collective-permute-done((bf16[128,1024]{1,0:T(8,128)(2,1)S(1)}, bf16[128,1024]{1,0:T(8,128)(2,1)S(1)}, u32[]{:S(2)}, u32[]{:S(2)}) %collective-permute-start.14) | collective-permute-done | bytes 262176 | tf_op jit(solution)/shard_map/ppermute | solution.py:214
  85.2 0.1 fusion.2
  85.3 1.9 %collective-permute-start.15 = (bf16[128,1024]{1,0:T(8,128)(2,1)S(1)}, bf16[128,1024]{1,0:T(8,128)(2,1)S(1)}, u32[]{:S(2)}, u32[]{:S(2)}) collective-permute-start(bf16[128,1024]{1,0:T(8,128)(2,1)S(1)} %fusion.2), channel_id=1, source_target_pairs={{8,0},{9,1},{12,4},{13,5},{16,8},{17,9},{20,12},{21,13},{24,16},{2... | collective-permute-start | bytes 786440 | tf_op jit(solution)/shard_map/ppermute | solution.py:214
  87.2 3.6 %collective-permute-done.12 = bf16[128,1024]{1,0:T(8,128)(2,1)S(1)} collective-permute-done((bf16[128,1024]{1,0:T(8,128)(2,1)S(1)}, bf16[128,1024]{1,0:T(8,128)(2,1)S(1)}, u32[]{:S(2)}, u32[]{:S(2)}) %collective-permute-start.12) | collective-permute-done | bytes 262176 | tf_op jit(solution)/shard_map/ppermute | solution.py:214
  90.8 0.1 fusion.3
  90.9 1.9 %collective-permute-start.13 = (bf16[128,1024]{1,0:T(8,128)(2,1)S(1)}, bf16[128,1024]{1,0:T(8,128)(2,1)S(1)}, u32[]{:S(2)}, u32[]{:S(2)}) collective-permute-start(bf16[128,1024]{1,0:T(8,128)(2,1)S(1)} %fusion.3), channel_id=1, source_target_pairs={{16,0},{17,1},{20,4},{21,5},{24,8},{25,9},{28,12},{29,13},{32,16},... | collective-permute-start | bytes 786440 | tf_op jit(solution)/shard_map/ppermute | solution.py:214
  92.8 2.8 %collective-permute-done.16 = bf16[128,1024]{1,0:T(8,128)(2,1)S(1)} collective-permute-done((bf16[128,1024]{1,0:T(8,128)(2,1)S(1)}, bf16[128,1024]{1,0:T(8,128)(2,1)S(1)}, u32[]{:S(2)}, u32[]{:S(2)}) %collective-permute-start.16) | collective-permute-done | bytes 262176 | tf_op jit(solution)/shard_map/ppermute | solution.py:214
  95.7 1.0 collective-permute-done.15
  96.7 5.9 %collective-permute-done.13 = bf16[128,1024]{1,0:T(8,128)(2,1)S(1)} collective-permute-done((bf16[128,1024]{1,0:T(8,128)(2,1)S(1)}, bf16[128,1024]{1,0:T(8,128)(2,1)S(1)}, u32[]{:S(2)}, u32[]{:S(2)}) %collective-permute-start.13) | collective-permute-done | bytes 262176 | tf_op jit(solution)/shard_map/ppermute | solution.py:214
  102.5 0.2 fusion.1
  102.7 0.7 fusion.4
  (5 shorter events, 0.1 us)
Async XLA Ops:
  2.5 39.1 %copy-start = (bf16[128,1024]{1,0:T(8,128)(2,1)}, bf16[128,1024]{1,0:T(8,128)(2,1)S(1)}, u32[]{:S(2)}) copy-start(bf16[128,1024]{1,0:T(8,128)(2,1)S(1)} %constant_dynamic-update-slice_fusion.x_ref) | copy-start | bytes 786436
  2.5 15.4 %collective-permute-start.7 = (bf16[128,1024]{1,0:T(8,128)(2,1)S(1)}, bf16[128,1024]{1,0:T(8,128)(2,1)S(1)}, u32[]{:S(2)}, u32[]{:S(2)}) collective-permute-start(bf16[128,1024]{1,0:T(8,128)(2,1)S(1)} %constant_dynamic-update-slice_fusion.x_ref), channel_id=1, source_target_pairs={{0,16},{1,17},{4,20},{5,21},{8,24},{9,25},{12,28},{13,29},{16,32},... | collective-permute-start | bytes 786440 | tf_op jit(solution)/shard_map/ppermute | solution.py:214
  7.3 16.6 %collective-permute-start.3 = (bf16[128,1024]{1,0:T(8,128)(2,1)S(1)}, bf16[128,1024]{1,0:T(8,128)(2,1)S(1)}, u32[]{:S(2)}, u32[]{:S(2)}) collective-permute-start(bf16[128,1024]{1,0:T(8,128)(2,1)S(1)} %constant_dynamic-update-slice_fusion.x_ref), channel_id=1, source_target_pairs={{0,8},{1,9},{4,12},{5,13},{8,16},{9,17},{12,20},{13,21},{16,24},{1... | collective-permute-start | bytes 786440 | tf_op jit(solution)/shard_map/ppermute | solution.py:214
  10.1 15.4 %collective-permute-start.1 = (bf16[128,1024]{1,0:T(8,128)(2,1)S(1)}, bf16[128,1024]{1,0:T(8,128)(2,1)S(1)}, u32[]{:S(2)}, u32[]{:S(2)}) collective-permute-start(bf16[128,1024]{1,0:T(8,128)(2,1)S(1)} %constant_dynamic-update-slice_fusion.x_ref), channel_id=1, source_target_pairs={{0,4},{1,5},{4,0},{5,1},{8,12},{9,13},{12,8},{13,9},{16,20},{17,21... | collective-permute-start | bytes 786440 | tf_op jit(solution)/shard_map/ppermute | solution.py:214
  11.1 17.6 %collective-permute-start = (bf16[128,1024]{1,0:T(8,128)(2,1)S(1)}, bf16[128,1024]{1,0:T(8,128)(2,1)S(1)}, u32[]{:S(2)}, u32[]{:S(2)}) collective-permute-start(bf16[128,1024]{1,0:T(8,128)(2,1)S(1)} %constant_dynamic-update-slice_fusion.x_ref), channel_id=1, source_target_pairs={{0,1},{1,0},{4,5},{5,4},{8,9},{9,8},{12,13},{13,12},{16,17},{17,16... | collective-permute-start | bytes 786440 | tf_op jit(solution)/shard_map/ppermute | solution.py:214
  17.9 23.6 %copy-start.1 = (bf16[128,1024]{1,0:T(8,128)(2,1)}, bf16[128,1024]{1,0:T(8,128)(2,1)S(1)}, u32[]{:S(2)}) copy-start(bf16[128,1024]{1,0:T(8,128)(2,1)S(1)} %collective-permute-done.7.y_refs_7_) | copy-start | bytes 786436
  17.9 16.5 %collective-permute-start.8 = (bf16[128,1024]{1,0:T(8,128)(2,1)S(1)}, bf16[128,1024]{1,0:T(8,128)(2,1)S(1)}, u32[]{:S(2)}, u32[]{:S(2)}) collective-permute-start(bf16[128,1024]{1,0:T(8,128)(2,1)S(1)} %collective-permute-done.7.y_refs_7_), channel_id=1, source_target_pairs={{0,1},{1,0},{4,5},{5,4},{8,9},{9,8},{12,13},{13,12},{16,17},{17,16... | collective-permute-start | bytes 786440 | tf_op jit(solution)/shard_map/ppermute | solution.py:214
  23.9 17.6 %copy-start.2 = (bf16[128,1024]{1,0:T(8,128)(2,1)}, bf16[128,1024]{1,0:T(8,128)(2,1)S(1)}, u32[]{:S(2)}) copy-start(bf16[128,1024]{1,0:T(8,128)(2,1)S(1)} %collective-permute-done.3.y_refs_3_) | copy-start | bytes 786436
  23.9 16.1 %collective-permute-start.4 = (bf16[128,1024]{1,0:T(8,128)(2,1)S(1)}, bf16[128,1024]{1,0:T(8,128)(2,1)S(1)}, u32[]{:S(2)}, u32[]{:S(2)}) collective-permute-start(bf16[128,1024]{1,0:T(8,128)(2,1)S(1)} %collective-permute-done.3.y_refs_3_), channel_id=1, source_target_pairs={{0,1},{1,0},{4,5},{5,4},{8,9},{9,8},{12,13},{13,12},{16,17},{17,16... | collective-permute-start | bytes 786440 | tf_op jit(solution)/shard_map/ppermute | solution.py:214
  25.5 14.6 %collective-permute-start.9 = (bf16[128,1024]{1,0:T(8,128)(2,1)S(1)}, bf16[128,1024]{1,0:T(8,128)(2,1)S(1)}, u32[]{:S(2)}, u32[]{:S(2)}) collective-permute-start(bf16[128,1024]{1,0:T(8,128)(2,1)S(1)} %collective-permute-done.7.y_refs_7_), channel_id=1, source_target_pairs={{0,4},{1,5},{4,0},{5,1},{8,12},{9,13},{12,8},{13,9},{16,20},{17,21... | collective-permute-start | bytes 786440 | tf_op jit(solution)/shard_map/ppermute | solution.py:214
  25.5 16.0 %copy-start.3 = (bf16[128,1024]{1,0:T(8,128)(2,1)}, bf16[128,1024]{1,0:T(8,128)(2,1)S(1)}, u32[]{:S(2)}) copy-start(bf16[128,1024]{1,0:T(8,128)(2,1)S(1)} %collective-permute-done.1.y_refs_1_) | copy-start | bytes 786436
  25.5 14.6 %collective-permute-start.5 = (bf16[128,1024]{1,0:T(8,128)(2,1)S(1)}, bf16[128,1024]{1,0:T(8,128)(2,1)S(1)}, u32[]{:S(2)}, u32[]{:S(2)}) collective-permute-start(bf16[128,1024]{1,0:T(8,128)(2,1)S(1)} %collective-permute-done.3.y_refs_3_), channel_id=1, source_target_pairs={{0,4},{1,5},{4,0},{5,1},{8,12},{9,13},{12,8},{13,9},{16,20},{17,21... | collective-permute-start | bytes 786440 | tf_op jit(solution)/shard_map/ppermute | solution.py:214
  28.7 12.8 %copy-start.4 = (bf16[128,1024]{1,0:T(8,128)(2,1)}, bf16[128,1024]{1,0:T(8,128)(2,1)S(1)}, u32[]{:S(2)}) copy-start(bf16[128,1024]{1,0:T(8,128)(2,1)S(1)} %collective-permute-done.y_refs_0_) | copy-start | bytes 786436
  28.7 11.4 %collective-permute-start.2 = (bf16[128,1024]{1,0:T(8,128)(2,1)S(1)}, bf16[128,1024]{1,0:T(8,128)(2,1)S(1)}, u32[]{:S(2)}, u32[]{:S(2)}) collective-permute-start(bf16[128,1024]{1,0:T(8,128)(2,1)S(1)} %collective-permute-done.y_refs_0_), channel_id=1, source_target_pairs={{0,4},{1,5},{4,0},{5,1},{8,12},{9,13},{12,8},{13,9},{16,20},{17,21... | collective-permute-start | bytes 786440 | tf_op jit(solution)/shard_map/ppermute | solution.py:214
  34.4 7.2 %copy-start.5 = (bf16[128,1024]{1,0:T(8,128)(2,1)}, bf16[128,1024]{1,0:T(8,128)(2,1)S(1)}, u32[]{:S(2)}) copy-start(bf16[128,1024]{1,0:T(8,128)(2,1)S(1)} %collective-permute-done.8.y_refs_8_) | copy-start | bytes 786436
  34.4 5.8 %collective-permute-start.10 = (bf16[128,1024]{1,0:T(8,128)(2,1)S(1)}, bf16[128,1024]{1,0:T(8,128)(2,1)S(1)}, u32[]{:S(2)}, u32[]{:S(2)}) collective-permute-start(bf16[128,1024]{1,0:T(8,128)(2,1)S(1)} %collective-permute-done.8.y_refs_8_), channel_id=1, source_target_pairs={{0,4},{1,5},{4,0},{5,1},{8,12},{9,13},{12,8},{13,9},{16,20},{17,21... | collective-permute-start | bytes 786440 | tf_op jit(solution)/shard_map/ppermute | solution.py:214
  40.0 1.6 %copy-start.6 = (bf16[128,1024]{1,0:T(8,128)(2,1)}, bf16[128,1024]{1,0:T(8,128)(2,1)S(1)}, u32[]{:S(2)}) copy-start(bf16[128,1024]{1,0:T(8,128)(2,1)S(1)} %collective-permute-done.4.y_refs_4_) | copy-start | bytes 786436
  40.0 1.5 %collective-permute-start.6 = (bf16[128,1024]{1,0:T(8,128)(2,1)S(1)}, bf16[128,1024]{1,0:T(8,128)(2,1)S(1)}, u32[]{:S(2)}, u32[]{:S(2)}) collective-permute-start(bf16[128,1024]{1,0:T(8,128)(2,1)S(1)} %collective-permute-done.4.y_refs_4_), channel_id=1, source_target_pairs={{0,4},{1,5},{4,0},{5,1},{8,12},{9,13},{12,8},{13,9},{16,20},{17,21... | collective-permute-start | bytes 786440 | tf_op jit(solution)/shard_map/ppermute | solution.py:214
  40.1 1.5 %copy-start.7 = (bf16[128,1024]{1,0:T(8,128)(2,1)}, bf16[128,1024]{1,0:T(8,128)(2,1)S(1)}, u32[]{:S(2)}) copy-start(bf16[128,1024]{1,0:T(8,128)(2,1)S(1)} %collective-permute-done.9.y_refs_9_) | copy-start | bytes 786436
  40.1 1.5 %copy-start.8 = (bf16[128,1024]{1,0:T(8,128)(2,1)}, bf16[128,1024]{1,0:T(8,128)(2,1)S(1)}, u32[]{:S(2)}) copy-start(bf16[128,1024]{1,0:T(8,128)(2,1)S(1)} %collective-permute-done.5.y_refs_5_) | copy-start | bytes 786436
  40.1 1.5 %copy-start.9 = (bf16[128,1024]{1,0:T(8,128)(2,1)}, bf16[128,1024]{1,0:T(8,128)(2,1)S(1)}, u32[]{:S(2)}) copy-start(bf16[128,1024]{1,0:T(8,128)(2,1)S(1)} %collective-permute-done.2.y_refs_2_) | copy-start | bytes 786436
  40.2 1.5 %copy-start.10 = (bf16[128,1024]{1,0:T(8,128)(2,1)}, bf16[128,1024]{1,0:T(8,128)(2,1)S(1)}, u32[]{:S(2)}) copy-start(bf16[128,1024]{1,0:T(8,128)(2,1)S(1)} %collective-permute-done.10.y_refs_10_) | copy-start | bytes 786436
  41.5 0.7 copy-start.11
  70.0 3.9 %collective-permute-start.11 = (bf16[3,2,128,1024]{3,2,1,0:T(8,128)(2,1)}, bf16[3,2,128,1024]{3,2,1,0:T(8,128)(2,1)S(1)}, u32[]{:S(2)}, u32[]{:S(2)}) collective-permute-start(bf16[3,2,128,1024]{3,2,1,0:T(8,128)(2,1)} %get-tuple-element.8), channel_id=1, source_target_pairs={{0,4},{1,5},{4,0},{5,1},{8,12},{9,13},{12,8},{13,9},{16,20},{17,21... | collective-permute-start | bytes 4718600 | tf_op jit(solution)/shard_map/ppermute | solution.py:214
  76.0 9.2 %collective-permute-start.14 = (bf16[128,1024]{1,0:T(8,128)(2,1)S(1)}, bf16[128,1024]{1,0:T(8,128)(2,1)S(1)}, u32[]{:S(2)}, u32[]{:S(2)}) collective-permute-start(bf16[128,1024]{1,0:T(8,128)(2,1)S(1)} %slice_bitcast_fusion.2), channel_id=1, source_target_pairs={{0,1},{1,0},{4,5},{5,4},{8,9},{9,8},{12,13},{13,12},{16,17},{17,16... | collective-permute-start | bytes 786440 | tf_op jit(solution)/shard_map/ppermute | solution.py:214
  77.4 13.4 %collective-permute-start.12 = (bf16[128,1024]{1,0:T(8,128)(2,1)S(1)}, bf16[128,1024]{1,0:T(8,128)(2,1)S(1)}, u32[]{:S(2)}, u32[]{:S(2)}) collective-permute-start(bf16[128,1024]{1,0:T(8,128)(2,1)S(1)} %slice_bitcast_fusion.4), channel_id=1, source_target_pairs={{0,1},{1,0},{4,5},{5,4},{8,9},{9,8},{12,13},{13,12},{16,17},{17,16... | collective-permute-start | bytes 786440 | tf_op jit(solution)/shard_map/ppermute | solution.py:214
  78.2 17.4 %collective-permute-start.16 = (bf16[128,1024]{1,0:T(8,128)(2,1)S(1)}, bf16[128,1024]{1,0:T(8,128)(2,1)S(1)}, u32[]{:S(2)}, u32[]{:S(2)}) collective-permute-start(bf16[128,1024]{1,0:T(8,128)(2,1)S(1)} %slice_bitcast_fusion), channel_id=1, source_target_pairs={{0,1},{1,0},{4,5},{5,4},{8,9},{9,8},{12,13},{13,12},{16,17},{17,16... | collective-permute-start | bytes 786440 | tf_op jit(solution)/shard_map/ppermute | solution.py:214
  85.3 11.4 %collective-permute-start.15 = (bf16[128,1024]{1,0:T(8,128)(2,1)S(1)}, bf16[128,1024]{1,0:T(8,128)(2,1)S(1)}, u32[]{:S(2)}, u32[]{:S(2)}) collective-permute-start(bf16[128,1024]{1,0:T(8,128)(2,1)S(1)} %fusion.2), channel_id=1, source_target_pairs={{8,0},{9,1},{12,4},{13,5},{16,8},{17,9},{20,12},{21,13},{24,16},{2... | collective-permute-start | bytes 786440 | tf_op jit(solution)/shard_map/ppermute | solution.py:214
  90.9 11.6 %collective-permute-start.13 = (bf16[128,1024]{1,0:T(8,128)(2,1)S(1)}, bf16[128,1024]{1,0:T(8,128)(2,1)S(1)}, u32[]{:S(2)}, u32[]{:S(2)}) collective-permute-start(bf16[128,1024]{1,0:T(8,128)(2,1)S(1)} %fusion.3), channel_id=1, source_target_pairs={{16,0},{17,1},{20,4},{21,5},{24,8},{25,9},{28,12},{29,13},{32,16},... | collective-permute-start | bytes 786440 | tf_op jit(solution)/shard_map/ppermute | solution.py:214
where the time goes:
time: 104 us; the launch traced here: 103 us
  waiting for transfers between devices  46.9 us (45%)
  Pallas kernels  27.8 us (27%)
  starting transfers between devices  22.3 us (21%)
  local copies, waits for them, and re-layouts  3.27 us (3%)
  other arithmetic  2.34 us (2%)
    ppermute x17, waiting for transfers between devices, sent(): return lax.ppermute(value, AXES, plan)  46.9 us
    pallas_call x1, Pallas kernels, attention(): pl.pallas_call(kernel, grid=(kv_heads,), in_specs=[pl.BlockSpec(lengths.s...  27.8 us
    ppermute x17, starting transfers between devices, sent(): return lax.ppermute(value, AXES, plan)  22.3 us
  transfers between devices with their start and end apart: 17, of which 12 were waited for; matrix products, arithmetic and copies ran while one was open for 0% of the time, Pallas kernels for 0%

commit v1 on v0

v1 whole, which is shorter than its diff:
```python
import math

import jax
import jax.numpy as jnp
from jax import lax
from jax.experimental import pallas as pl
from jax.experimental.pallas import tpu as pltpu
from jax.sharding import PartitionSpec as P

HD = 128
AXES = ("ctx", "kv")
BACK = 8
NEG = -1e30
NT = (((1,), (1,)), ((), ()))
SCALE = 1.0 / math.sqrt(HD)
SCALE_LOG2 = math.log2(math.e) / math.sqrt(HD)


def device_of(n_ctx, group, core, part):
    if group < n_ctx // 2:
        return (2 * group + core) * 4 + part
    return (2 * (n_ctx - 1 - group) + core) * 4 + part + 2


def pairs(n_ctx, move):
    found = []
    for group in range(n_ctx):
        for core in range(2):
            for part in range(2):
                target = move(group, core, part)
                if 0 <= target[0] < n_ctx:
                    found.append((device_of(n_ctx, group, core, part), device_of(n_ctx, *target)))
    return found


def ahead(n_ctx, steps):
    def move(group, core, part):
        crosses = (group < n_ctx // 2) != (group + steps < n_ctx // 2)
        return group + steps, core, part ^ int(crosses)

    return pairs(n_ctx, move)


def heads_of(ref, cols):
    return ref[:, pl.ds(pl.multiple_of(cols, HD), HD)]


def split_kernel(keys_ref, values_ref, mine_ref, send_ref):
    core = lax.axis_index("ctx") % 2
    kept = mine_ref.shape[1] // (2 * HD)
    for ref, side in ((mine_ref, core), (send_ref, 1 - core)):
        for a in range(kept):
            cols = (side * kept + a) * HD
            ref[:, 2 * a * HD : (2 * a + 1) * HD] = heads_of(keys_ref, cols)
            ref[:, (2 * a + 1) * HD : (2 * a + 2) * HD] = heads_of(values_ref, cols)


def merge_kernel(mine_ref, got_ref, key_ref, value_ref):
    core = lax.axis_index("ctx") % 2
    kept = mine_ref.shape[1] // (2 * HD)
    for ref, side in ((mine_ref, core), (got_ref, 1 - core)):
        for a in range(kept):
            cols = pl.ds(pl.multiple_of((side * kept + a) * HD, HD), HD)
            key_ref[:, cols] = ref[:, 2 * a * HD : (2 * a + 1) * HD]
            value_ref[:, cols] = ref[:, (2 * a + 1) * HD : (2 * a + 2) * HD]


def kernel(
    lengths_ref, q_own_ref, q_got_ref, g_own_ref, g_got_ref, pieces, dq_mine_ref, dq_send_ref, parts,
    win, acc, s_scr, pp_scr, dp_scr, p_scr, ds_scr, q_ref, g_ref, dq_ref,
):
    step = pl.program_id(1)
    rows = q_ref.shape[0]
    heads = q_ref.shape[1] // HD
    width = (BACK + 1) * rows
    n_ctx = lax.axis_size("ctx")
    turn = n_ctx // 2
    slot = lax.axis_index("ctx")
    lane = lax.axis_index("kv")
    upper = lane // 2
    part = lane % 2
    group = jnp.where(upper == 0, slot // 2, n_ctx - 1 - slot // 2)
    mine = (slot % 2) ^ step

    @pl.when(step == 0)
    def _():
        q_ref[...] = q_own_ref[...]
        g_ref[...] = g_own_ref[...]

    @pl.when(step == 1)
    def _():
        q_ref[...] = q_got_ref[...]
        g_ref[...] = g_got_ref[...]

    def spot(which, y_rel, core):
        crossed = jnp.where((group >= turn) & (group < turn + 2 - which), 1, 0)
        index = 4 * which + 2 * (core ^ upper ^ crossed) + (part ^ y_rel ^ crossed)
        return pl.ds(pl.multiple_of(index * rows, rows), rows)

    spots = [(which, y_rel, core) for which in range(3) for y_rel in range(2) for core in range(2)]

    @pl.when(step == 0)
    def _():
        acc[...] = jnp.zeros_like(acc)
        for which, y_rel, core in spots:
            win[spot(which, y_rel, core), :] = pieces[2 * which + y_rel][core * rows : (core + 1) * rows, :]

    first = 2 * (mine ^ upper) + part
    lens = lengths_ref[...].astype(jnp.float32)
    docs = lens.shape[1]
    below = lax.broadcasted_iota(jnp.int32, (docs, docs), 1) <= lax.broadcasted_iota(jnp.int32, (docs, docs), 0)
    ends = jnp.sum(jnp.where(below, lens, 0.0), axis=1, keepdims=True)
    start = (4 * group + first) * rows
    pos = (start + lax.broadcasted_iota(jnp.int32, (1, rows), 1)).astype(jnp.float32)
    lo = jnp.max(jnp.where(ends <= pos, ends, 0.0), axis=0, keepdims=True).astype(jnp.int32)
    lo = lo - (start - BACK * rows)
    lo2 = jnp.concatenate([lo, lo], axis=1)
    base = first * rows
    window = pl.ds(pl.multiple_of(base, rows), width)
    keys_t = win[window, :HD].T
    column = lax.broadcasted_iota(jnp.int32, (1, 2 * rows), 1) % rows

    def key_rows(t):
        return pl.ds(pl.multiple_of(base + t * rows, rows), rows)

    def head(ref, index):
        return ref[:, index * HD : (index + 1) * HD]

    def folded(tile, fold):
        return fold(tile.reshape(rows // 8, 8, 2 * rows), axis=0)

    pair_count = heads // 2
    state = {}

    def pair_of(ref, hp):
        return jnp.concatenate([head(ref, 2 * hp), head(ref, 2 * hp + 1)], axis=0)

    def score_tile(hp, t):
        tile = lax.dot_general(
            win[key_rows(t), :HD], pair_of(q_ref, hp), NT, preferred_element_type=jnp.float32
        )
        key_row = lax.broadcasted_iota(jnp.int32, (rows, 2 * rows), 0) + t * rows
        allowed = key_row >= lo2
        if t == BACK:
            allowed = allowed & (key_row - BACK * rows <= column)
        tile = jnp.where(allowed, tile, NEG)
        s_scr[hp, t * rows : (t + 1) * rows, :] = tile
        peak = folded(tile, jnp.max)
        state["top", hp] = peak if t == 0 else jnp.maximum(state["top", hp], peak)

    def weight_tile(hp, t):
        here = slice(t * rows, (t + 1) * rows)
        if t == 0:
            state["top", hp] = jnp.max(state["top", hp], axis=0, keepdims=True) * SCALE_LOG2
            state["total", hp] = state["dots", hp] = jnp.zeros((8, 2 * rows), jnp.float32)
        weight = jnp.exp2(s_scr[hp, here, :] * SCALE_LOG2 - state["top", hp])
        grad_prob = lax.dot_general(
            win[key_rows(t), HD:], pair_of(g_ref, hp), NT, preferred_element_type=jnp.float32
        )
        pp_scr[hp, here, :] = weight
        dp_scr[hp, here, :] = grad_prob
        state["total", hp] += folded(weight, jnp.sum)
        state["dots", hp] += folded(weight * grad_prob, jnp.sum)

    def prob_tile(hp, t):
        here = slice(t * rows, (t + 1) * rows)
        lanes = slice(hp * 2 * rows, (hp + 1) * 2 * rows)
        if t == 0:
            state["inverse", hp] = 1.0 / jnp.sum(state["total", hp], axis=0, keepdims=True)
            state["delta", hp] = jnp.sum(state["dots", hp], axis=0, keepdims=True) * state["inverse", hp]
        prob = pp_scr[hp, here, :] * state["inverse", hp]
        p_scr[here, lanes] = prob.astype(jnp.bfloat16)
        ds_scr[here, lanes] = (prob * (dp_scr[hp, here, :] - state["delta", hp])).astype(jnp.bfloat16)

    def products(hp):
        lanes = slice(hp * 2 * rows, (hp + 1) * 2 * rows)
        dq = jnp.dot(keys_t, ds_scr[:, lanes], preferred_element_type=jnp.float32).T * SCALE
        dq = dq.astype(jnp.bfloat16)
        dq_ref[:, 2 * hp * HD : (2 * hp + 1) * HD] = dq[:rows]
        dq_ref[:, (2 * hp + 1) * HD : (2 * hp + 2) * HD] = dq[rows:]
        acc[window, :HD] += (
            jnp.dot(ds_scr[:, lanes], pair_of(q_ref, hp), preferred_element_type=jnp.float32) * SCALE
        )
        acc[window, HD:] += jnp.dot(p_scr[:, lanes], pair_of(g_ref, hp), preferred_element_type=jnp.float32)

    for t in range(BACK + 1):
        score_tile(0, t)
    for hp in range(pair_count):
        for t in range(BACK + 1):
            weight_tile(hp, t)
        if hp > 0:
            products(hp - 1)
        for t in range(BACK + 1):
            if hp + 1 < pair_count:
                score_tile(hp + 1, t)
            prob_tile(hp, t)
    products(pair_count - 1)

    @pl.when(step == 0)
    def _():
        dq_mine_ref[...] = dq_ref[...]

    @pl.when(step == 1)
    def _():
        dq_send_ref[...] = dq_ref[...]
        for which, y_rel, core in spots:
            parts[2 * which + y_rel][core * rows : (core + 1) * rows, :] = acc[
                spot(which, y_rel, core), :
            ].astype(jnp.bfloat16)


def attention(lengths, queries, q_got, grad_out, g_got, pieces):
    rows, q_width = q_got.shape
    kv_heads = pieces[0].shape[1] // (2 * HD)
    span = q_width // kv_heads
    heads = span // HD
    width = (BACK + 1) * rows
    by_core = pl.BlockSpec((rows, span), lambda a, r: (0, kv_heads * (lax.axis_index("ctx") % 2) + a))
    by_head = pl.BlockSpec((rows, span), lambda a, r: (0, a))
    piece = pl.BlockSpec((2 * rows, 2 * HD), lambda a, r: (0, a))
    tile = pltpu.VMEM((heads // 2, width, 2 * rows), jnp.float32)
    flat = pltpu.VMEM((width, heads * rows), jnp.bfloat16)
    block = pltpu.VMEM((rows, span), jnp.bfloat16)
    half = jax.ShapeDtypeStruct((rows, q_width), jnp.bfloat16)
    return pl.pallas_call(
        kernel,
        grid=(kv_heads, 2),
        in_specs=[
            pl.BlockSpec(lengths.shape, lambda a, r: (0, 0)),
            by_core,
            by_head,
            by_core,
            by_head,
            [piece] * 6,
        ],
        out_specs=[by_head, by_head, [piece] * 6],
        out_shape=[half, half, [jax.ShapeDtypeStruct(pieces[0].shape, jnp.bfloat16)] * 6],
        scratch_shapes=[
            pltpu.VMEM((12 * rows, 2 * HD), jnp.bfloat16),
            pltpu.VMEM((12 * rows, 2 * HD), jnp.float32),
            tile,
            tile,
            tile,
            flat,
            flat,
            block,
            block,
            block,
        ],
        compiler_params=pltpu.CompilerParams(vmem_limit_bytes=56 * 2**20),
    )(lengths, queries, q_got, grad_out, g_got, pieces)


def body(queries, keys, values, grad_out, doc_lengths):
    n_ctx = lax.axis_size("ctx")
    core = lax.axis_index("ctx") % 2
    swap_part = pairs(n_ctx, lambda g, c, y: (g, c, 1 - y))
    swap_core = pairs(n_ctx, lambda g, c, y: (g, 1 - c, y))
    rows, kv_width = keys.shape

    def sent(value, plan):
        return lax.ppermute(value, AXES, plan)

    def other_heads(value):
        half = value.shape[1] // 2
        return sent(lax.dynamic_slice_in_dim(value, (1 - core) * half, half, 1), swap_core)

    def in_order(mine, got, axis):
        return jnp.where(
            core == 0, jnp.concatenate([mine, got], axis=axis), jnp.concatenate([got, mine], axis=axis)
        )

    def added(*terms):
        return sum(term.astype(jnp.float32) for term in terms)

    chunk = jax.ShapeDtypeStruct(keys.shape, jnp.bfloat16)
    mine, given = pl.pallas_call(split_kernel, out_shape=[chunk, chunk])(keys, values)
    own = in_order(mine, sent(given, swap_core), 0)
    pieces = []
    for which in range(3):
        mine = own if which == 2 else sent(own, ahead(n_ctx, 2 - which))
        pieces += [mine, sent(mine, swap_part)]
    dq_mine, dq_send, parts = attention(
        doc_lengths.reshape(1, -1), queries, other_heads(queries), grad_out, other_heads(grad_out), pieces
    )
    query_grad = in_order(dq_mine, sent(dq_send, swap_core), 1)
    total = None
    for which in range(3):
        summed = added(parts[2 * which], sent(parts[2 * which + 1], swap_part))
        if which < 2:
            summed = sent(summed.astype(jnp.bfloat16), ahead(n_ctx, which - 2)).astype(jnp.float32)
        total = summed if total is None else total + summed
    total = total.astype(jnp.bfloat16)
    given = lax.dynamic_slice_in_dim(total, (1 - core) * rows, rows, 0)
    mine = lax.dynamic_slice_in_dim(total, core * rows, rows, 0)
    key_grad, value_grad = pl.pallas_call(merge_kernel, out_shape=[chunk, chunk])(mine, sent(given, swap_core))
    return query_grad, key_grad, value_grad


def solution(mesh):
    rows = P(AXES, None)
    return jax.shard_map(
        body,
        mesh=mesh,
        in_specs=(rows, rows, rows, rows, P()),
        out_specs=(rows, rows, rows),
        check_vma=False,
    )
```

time: 104 us -> 90.3 us (0.87)
  waiting for transfers between devices: 46.9 us -> 35.4 us
  starting transfers between devices: 22.3 us -> 19.9 us
  Pallas kernels: 27.8 us -> 26.2 us
  other arithmetic: 2.34 us -> 3.44 us
    ppermute x17 -> x15, waiting for transfers between devices: 46.9 us -> 35.4 us  [sent(): return lax.ppermute(value, AXES, plan)]
    ppermute x17 -> x15, starting transfers between devices: 22.3 us -> 19.9 us  [sent(): return lax.ppermute(value, AXES, plan)]
    convert_element_type x1 -> x0, other arithmetic: 2.04 us -> none  [body(): both = added(keep[which], got[which]).astype(jnp.bfloat16)]
    convert_element_type x2, other arithmetic: 0.13 us -> 2.03 us  [body(): summed.astype(jnp.bfloat16)]
    dynamic_slice x0 -> x3, local copies, waits for them, and re-layouts: none -> 1.82 us  [the longest x2 1.15 us: other_heads(): lax.dynamic_slice_in_dim(value, (1 - core) * half, half, 1)]
    pallas_call x1 -> x3, Pallas kernels: 27.8 us -> 26.2 us  [the longest x1 22.7 us: attention(): pl.pallas_call(kernel, grid=(kv_heads, 2), in_specs=[pl.BlockSpec(lengths...]
    select_n x0 -> x2, other arithmetic: none -> 1.27 us  [in_order(): jnp.where(core == 0, jnp.concatenate([mine, got], axis=axis), jnp.concate...]
  transfers between devices with their start and end apart: 17 -> 15, of which waited for: 12 -> 10; matrix products, arithmetic and copies ran while one was open for 0% -> 6% of each run, Pallas kernels for 0% -> 0%
where the time goes in v1:
time: 90.3 us; the launch traced here: 89 us
  waiting for transfers between devices  35.4 us (39%)
  Pallas kernels  26.2 us (29%)
  starting transfers between devices  19.9 us (22%)
  other arithmetic  3.44 us (4%)
  local copies, waits for them, and re-layouts  3.19 us (4%)
    ppermute x15, waiting for transfers between devices, sent(): return lax.ppermute(value, AXES, plan)  35.4 us
    pallas_call x1, Pallas kernels, attention(): pl.pallas_call(kernel, grid=(kv_heads, 2), in_specs=[pl.BlockSpec(lengths...  22.7 us
    ppermute x15, starting transfers between devices, sent(): return lax.ppermute(value, AXES, plan)  19.9 us
    convert_element_type x2, other arithmetic, body(): summed.astype(jnp.bfloat16)  2.03 us
  transfers between devices with their start and end apart: 15, of which 10 were waited for; matrix products, arithmetic and copies ran while one was open for 6% of the time, Pallas kernels for 0%

profile of v1, /device:TPU:230, one launch (start us, length us, event | category | flops | bytes accessed | tf_op | source)
XLA Modules:
  0.0 89.0 jit_solution(326560036885567293)
XLA Ops:
  0.6 0.0 copy-start
  0.6 1.8 %shard_map.76 = (bf16[128,512]{1,0:T(8,128)(2,1)}, bf16[128,512]{1,0:T(8,128)(2,1)}) custom-call(bf16[128,512]{1,0:T(8,128)(2,1)} %keys_ref.1, bf16[128,512]{1,0:T(8,128)(2,1)} %values_ref.1), custom_call_target="tpu_custom_call" | custom-call | tf_op jit(solution)/shard_map/pallas_call | solution.py:277
  2.4 0.0 collective-permute-start.2
  2.4 0.0 copy-start.11
  2.4 1.1 %constant_dynamic-slice_fusion.2 = bf16[128,2048]{1,0:T(8,128)(2,1)S(1)} fusion(bf16[128,4096]{1,0:T(8,128)(2,1)} %g_own_ref.1, s32[]{:T(128)S(6)} %select_n.35), kind=kLoop, calls=%fused_computation.7 | loop fusion | bytes 1048580 | tf_op jit(solution)/shard_map/dynamic_slice | solution.py:266
  3.6 0.6 collective-permute-start.1
  4.2 0.0 copy-done
  4.2 0.0 collective-permute-done.2
  4.2 0.0 copy-done.11
  4.2 0.1 maximum_select_fusion.1.pieces_4_
  4.3 0.0 copy-start.1
  4.3 4.9 %collective-permute-start.5 = (bf16[256,512]{1,0:T(8,128)(2,1)S(1)}, bf16[256,512]{1,0:T(8,128)(2,1)S(1)}, u32[]{:S(2)}, u32[]{:S(2)}) collective-permute-start(bf16[256,512]{1,0:T(8,128)(2,1)S(1)} %maximum_select_fusion.1.pieces_4_), channel_id=1, source_target_pairs={{0,8},{1,9},{4,12},{5,13},{8,16},{9,17},{12,20},{13,21},{16,24},{1... | collective-permute-start | bytes 786440 | tf_op jit(solution)/shard_map/ppermute | solution.py:262
  9.2 0.1 collective-permute-start
  9.3 2.7 %collective-permute-start.3 = (bf16[256,512]{1,0:T(8,128)(2,1)S(1)}, bf16[256,512]{1,0:T(8,128)(2,1)S(1)}, u32[]{:S(2)}, u32[]{:S(2)}) collective-permute-start(bf16[256,512]{1,0:T(8,128)(2,1)S(1)} %maximum_select_fusion.1.pieces_4_), channel_id=1, source_target_pairs={{0,16},{1,17},{4,20},{5,21},{8,24},{9,25},{12,28},{13,29},{16,32},... | collective-permute-start | bytes 786440 | tf_op jit(solution)/shard_map/ppermute | solution.py:262
  12.0 0.2 collective-permute-start.7
  12.3 8.7 %collective-permute-done.5.pieces_2_ = bf16[256,512]{1,0:T(8,128)(2,1)S(1)} collective-permute-done((bf16[256,512]{1,0:T(8,128)(2,1)S(1)}, bf16[256,512]{1,0:T(8,128)(2,1)S(1)}, u32[]{:S(2)}, u32[]{:S(2)}) %collective-permute-start.5) | collective-permute-done | bytes 262176 | tf_op jit(solution)/shard_map/ppermute | solution.py:262
  21.0 0.0 copy-start.6
  21.0 1.6 %collective-permute-start.6 = (bf16[256,512]{1,0:T(8,128)(2,1)S(1)}, bf16[256,512]{1,0:T(8,128)(2,1)S(1)}, u32[]{:S(2)}, u32[]{:S(2)}) collective-permute-start(bf16[256,512]{1,0:T(8,128)(2,1)S(1)} %collective-permute-done.5.pieces_2_), channel_id=1, source_target_pairs={{0,1},{1,0},{4,5},{5,4},{8,9},{9,8},{12,13},{13,12},{16,17},{17,16... | collective-permute-start | bytes 786440 | tf_op jit(solution)/shard_map/ppermute | solution.py:262
  22.5 1.3 %collective-permute-done.3.pieces_0_ = bf16[256,512]{1,0:T(8,128)(2,1)S(1)} collective-permute-done((bf16[256,512]{1,0:T(8,128)(2,1)S(1)}, bf16[256,512]{1,0:T(8,128)(2,1)S(1)}, u32[]{:S(2)}, u32[]{:S(2)}) %collective-permute-start.3) | collective-permute-done | bytes 262176 | tf_op jit(solution)/shard_map/ppermute | solution.py:262
  23.8 0.0 copy-start.7
  23.9 0.1 collective-permute-start.4
  24.0 0.0 collective-permute-done.7.pieces_5_
  24.0 0.0 collective-permute-done.1.g_got_ref
  24.0 0.0 copy-start.3
  24.0 0.0 collective-permute-done.q_got_ref
  24.0 0.0 copy-start.4
  24.0 4.8 %collective-permute-done.6.pieces_3_ = bf16[256,512]{1,0:T(8,128)(2,1)S(1)} collective-permute-done((bf16[256,512]{1,0:T(8,128)(2,1)S(1)}, bf16[256,512]{1,0:T(8,128)(2,1)S(1)}, u32[]{:S(2)}, u32[]{:S(2)}) %collective-permute-start.6) | collective-permute-done | bytes 262176 | tf_op jit(solution)/shard_map/ppermute | solution.py:262
  28.9 4.1 %collective-permute-done.4.pieces_1_ = bf16[256,512]{1,0:T(8,128)(2,1)S(1)} collective-permute-done((bf16[256,512]{1,0:T(8,128)(2,1)S(1)}, bf16[256,512]{1,0:T(8,128)(2,1)S(1)}, u32[]{:S(2)}, u32[]{:S(2)}) %collective-permute-start.4) | collective-permute-done | bytes 262176 | tf_op jit(solution)/shard_map/ppermute | solution.py:262
  33.0 0.0 copy-done.1
  33.0 0.0 copy-done.6
  33.0 0.0 copy-done.7
  33.0 0.0 copy-done.8
  33.0 0.0 copy-done.3
  33.0 0.0 copy-done.4
  33.0 0.0 copy-done.9
  33.0 0.7 copy-done.10
  33.7 22.7 %shard_map.77 = (bf16[128,2048]{1,0:T(8,128)(2,1)}, bf16[128,2048]{1,0:T(8,128)(2,1)}, bf16[256,512]{1,0:T(8,128)(2,1)}, bf16[256,512]{1,0:T(8,128)(2,1)}, bf16[...) custom-call(s32[1,64]{1,0:T(1,128)} %bitcast.1, ...), custom_call_target="tpu_custom_call" | custom-call | tf_op jit(solution)/shard_map/pallas_call | solution.py:225
  56.4 0.0 copy-start.13
  56.4 0.0 copy-start.5
  56.4 1.7 %collective-permute-start.9 = (bf16[256,512]{1,0:T(8,128)(2,1)}, bf16[256,512]{1,0:T(8,128)(2,1)S(1)}, u32[]{:S(2)}, u32[]{:S(2)}) collective-permute-start(bf16[256,512]{1,0:T(8,128)(2,1)} %get-tuple-element.20), channel_id=1, source_target_pairs={{0,1},{1,0},{4,5},{5,4},{8,9},{9,8},{12,13},{13,12},{16,17},{17,16... | collective-permute-start | bytes 786440 | tf_op jit(solution)/shard_map/ppermute | solution.py:262
  58.1 0.4 collective-permute-start.11
  58.5 1.6 %collective-permute-start.13 = (bf16[256,512]{1,0:T(8,128)(2,1)}, bf16[256,512]{1,0:T(8,128)(2,1)S(1)}, u32[]{:S(2)}, u32[]{:S(2)}) collective-permute-start(bf16[256,512]{1,0:T(8,128)(2,1)} %get-tuple-element.24), channel_id=1, source_target_pairs={{0,1},{1,0},{4,5},{5,4},{8,9},{9,8},{12,13},{13,12},{16,17},{17,16... | collective-permute-start | bytes 786440 | tf_op jit(solution)/shard_map/ppermute | solution.py:262
  60.1 5.8 %collective-permute-done.9 = bf16[256,512]{1,0:T(8,128)(2,1)S(1)} collective-permute-done((bf16[256,512]{1,0:T(8,128)(2,1)}, bf16[256,512]{1,0:T(8,128)(2,1)S(1)}, u32[]{:S(2)}, u32[]{:S(2)}) %collective-permute-start.9) | collective-permute-done | bytes 262176 | tf_op jit(solution)/shard_map/ppermute | solution.py:262
  66.0 1.0 %add_convert_fusion.2 = bf16[256,512]{1,0:T(8,128)(2,1)S(1)} fusion(bf16[256,512]{1,0:T(8,128)(2,1)S(1)} %collective-permute-done.9, bf16[256,512]{1,0:T(8,128)(2,1)} %get-tuple-element.19), kind=kLoop, calls=%fused_computation.3 | loop fusion | flops 524288 | bytes 786432 | tf_op jit(solution)/shard_map/convert_element_type | solution.py:291
  67.0 3.5 %collective-permute-start.10 = (bf16[256,512]{1,0:T(8,128)(2,1)S(1)}, bf16[256,512]{1,0:T(8,128)(2,1)S(1)}, u32[]{:S(2)}, u32[]{:S(2)}) collective-permute-start(bf16[256,512]{1,0:T(8,128)(2,1)S(1)} %add_convert_fusion.2), channel_id=1, source_target_pairs={{16,0},{17,1},{20,4},{21,5},{24,8},{25,9},{28,12},{29,13},{32,16},... | collective-permute-start | bytes 786440 | tf_op jit(solution)/shard_map/ppermute | solution.py:262
  70.5 1.1 %collective-permute-done.11 = bf16[256,512]{1,0:T(8,128)(2,1)S(1)} collective-permute-done((bf16[256,512]{1,0:T(8,128)(2,1)}, bf16[256,512]{1,0:T(8,128)(2,1)S(1)}, u32[]{:S(2)}, u32[]{:S(2)}) %collective-permute-start.11) | collective-permute-done | bytes 262176 | tf_op jit(solution)/shard_map/ppermute | solution.py:262
  71.6 1.0 %add_convert_fusion.1 = bf16[256,512]{1,0:T(8,128)(2,1)S(1)} fusion(bf16[256,512]{1,0:T(8,128)(2,1)S(1)} %collective-permute-done.11, bf16[256,512]{1,0:T(8,128)(2,1)} %get-tuple-element.21), kind=kLoop, calls=%fused_computation.2 | loop fusion | flops 524288 | bytes 786432 | tf_op jit(solution)/shard_map/convert_element_type | solution.py:291
  72.6 0.0 copy-start.2
  72.6 2.4 %collective-permute-start.12 = (bf16[256,512]{1,0:T(8,128)(2,1)S(1)}, bf16[256,512]{1,0:T(8,128)(2,1)S(1)}, u32[]{:S(2)}, u32[]{:S(2)}) collective-permute-start(bf16[256,512]{1,0:T(8,128)(2,1)S(1)} %add_convert_fusion.1), channel_id=1, source_target_pairs={{8,0},{9,1},{12,4},{13,5},{16,8},{17,9},{20,12},{21,13},{24,16},{2... | collective-permute-start | bytes 786440 | tf_op jit(solution)/shard_map/ppermute | solution.py:262
  75.0 0.0 copy-done.13
  75.0 0.1 collective-permute-start.8
  75.1 0.2 collective-permute-done.13
  75.3 7.4 %collective-permute-done.10 = bf16[256,512]{1,0:T(8,128)(2,1)S(1)} collective-permute-done((bf16[256,512]{1,0:T(8,128)(2,1)S(1)}, bf16[256,512]{1,0:T(8,128)(2,1)S(1)}, u32[]{:S(2)}, u32[]{:S(2)}) %collective-permute-start.10) | collective-permute-done | bytes 262176 | tf_op jit(solution)/shard_map/ppermute | solution.py:262
  82.7 1.7 %collective-permute-done.12 = bf16[256,512]{1,0:T(8,128)(2,1)S(1)} collective-permute-done((bf16[256,512]{1,0:T(8,128)(2,1)S(1)}, bf16[256,512]{1,0:T(8,128)(2,1)S(1)}, u32[]{:S(2)}, u32[]{:S(2)}) %collective-permute-start.12) | collective-permute-done | bytes 262176 | tf_op jit(solution)/shard_map/ppermute | solution.py:262
  84.5 0.0 copy-done.5
  84.5 0.1 add_convert_fusion
  84.6 0.7 constant_dynamic-slice_fusion
  85.3 0.0 collective-permute-start.14
  85.3 0.0 collective-permute-done.8
  85.3 0.0 copy-done.2
  85.3 1.2 %maximum_select_fusion = bf16[128,4096]{1,0:T(8,128)(2,1)} fusion(bf16[128,2048]{1,0:T(8,128)(2,1)S(1)} %collective-permute-done.8, bf16[128,2048]{1,0:T(8,128)(2,1)S(1)} %copy-done.2, pred[]{:T(512)S(6)} %eq.6), kind=kLoop, calls=%fused_computation | loop fusion | flops 4718592 | bytes 2097153 | tf_op jit(solution)/shard_map/jit(_where)/select_n | solution.py:269
  86.5 0.1 collective-permute-done.14.got_ref
  86.6 0.7 copy-done.12
  87.3 1.7 %shard_map.78 = (bf16[128,512]{1,0:T(8,128)(2,1)}, bf16[128,512]{1,0:T(8,128)(2,1)}) custom-call(bf16[128,512]{1,0:T(8,128)(2,1)} %get-tuple-element.28.mine_ref, bf16[128,512]{1,0:T(8,128)(2,1)} %copy-done.12), custom_call_target="tpu_custom_call" | custom-call | tf_op jit(solution)/shard_map/pallas_call | solution.py:296
  (5 shorter events, 0.0 us)
Async XLA Ops:
  0.6 3.5 %copy-start = (bf16[128,4096]{1,0:T(8,128)(2,1)S(1)}, bf16[128,4096]{1,0:T(8,128)(2,1)}, u32[]{:S(2)}) copy-start(bf16[128,4096]{1,0:T(8,128)(2,1)} %q_own_ref.1) | copy-start | bytes 3145732
  2.4 1.8 %collective-permute-start.2 = (bf16[128,512]{1,0:T(8,128)(2,1)}, bf16[128,512]{1,0:T(8,128)(2,1)S(1)}, u32[]{:S(2)}, u32[]{:S(2)}) collective-permute-start(bf16[128,512]{1,0:T(8,128)(2,1)} %get-tuple-element.16), channel_id=1, source_target_pairs={{0,4},{1,5},{4,0},{5,1},{8,12},{9,13},{12,8},{13,9},{16,20},{17,21... | collective-permute-start | bytes 393224 | tf_op jit(solution)/shard_map/ppermute | solution.py:262
  2.4 1.8 %copy-start.11 = (bf16[128,512]{1,0:T(8,128)(2,1)S(1)}, bf16[128,512]{1,0:T(8,128)(2,1)}, u32[]{:S(2)}) copy-start(bf16[128,512]{1,0:T(8,128)(2,1)} %get-tuple-element.15) | copy-start | bytes 393220
  3.6 20.4 %collective-permute-start.1 = (bf16[128,2048]{1,0:T(8,128)(2,1)S(1)}, bf16[128,2048]{1,0:T(8,128)(2,1)S(1)}, u32[]{:S(2)}, u32[]{:S(2)}) collective-permute-start(bf16[128,2048]{1,0:T(8,128)(2,1)S(1)} %constant_dynamic-slice_fusion.2), channel_id=1, source_target_pairs={{0,4},{1,5},{4,0},{5,1},{8,12},{9,13},{12,8},{13,9},{16,20},{17,21... | collective-permute-start | bytes 1572872 | tf_op jit(solution)/shard_map/ppermute | solution.py:262
  4.3 28.7 %copy-start.1 = (bf16[256,512]{1,0:T(8,128)(2,1)}, bf16[256,512]{1,0:T(8,128)(2,1)S(1)}, u32[]{:S(2)}) copy-start(bf16[256,512]{1,0:T(8,128)(2,1)S(1)} %maximum_select_fusion.1.pieces_4_) | copy-start | bytes 786436
  4.3 16.7 %collective-permute-start.5 = (bf16[256,512]{1,0:T(8,128)(2,1)S(1)}, bf16[256,512]{1,0:T(8,128)(2,1)S(1)}, u32[]{:S(2)}, u32[]{:S(2)}) collective-permute-start(bf16[256,512]{1,0:T(8,128)(2,1)S(1)} %maximum_select_fusion.1.pieces_4_), channel_id=1, source_target_pairs={{0,8},{1,9},{4,12},{5,13},{8,16},{9,17},{12,20},{13,21},{16,24},{1... | collective-permute-start | bytes 786440 | tf_op jit(solution)/shard_map/ppermute | solution.py:262
  9.2 14.8 %collective-permute-start = (bf16[128,2048]{1,0:T(8,128)(2,1)S(1)}, bf16[128,2048]{1,0:T(8,128)(2,1)S(1)}, u32[]{:S(2)}, u32[]{:S(2)}) collective-permute-start(bf16[128,2048]{1,0:T(8,128)(2,1)S(1)} %constant_dynamic-slice_fusion.3), channel_id=1, source_target_pairs={{0,4},{1,5},{4,0},{5,1},{8,12},{9,13},{12,8},{13,9},{16,20},{17,21... | collective-permute-start | bytes 1572872 | tf_op jit(solution)/shard_map/ppermute | solution.py:262
  9.3 14.5 %collective-permute-start.3 = (bf16[256,512]{1,0:T(8,128)(2,1)S(1)}, bf16[256,512]{1,0:T(8,128)(2,1)S(1)}, u32[]{:S(2)}, u32[]{:S(2)}) collective-permute-start(bf16[256,512]{1,0:T(8,128)(2,1)S(1)} %maximum_select_fusion.1.pieces_4_), channel_id=1, source_target_pairs={{0,16},{1,17},{4,20},{5,21},{8,24},{9,25},{12,28},{13,29},{16,32},... | collective-permute-start | bytes 786440 | tf_op jit(solution)/shard_map/ppermute | solution.py:262
  12.0 12.0 %collective-permute-start.7 = (bf16[256,512]{1,0:T(8,128)(2,1)S(1)}, bf16[256,512]{1,0:T(8,128)(2,1)S(1)}, u32[]{:S(2)}, u32[]{:S(2)}) collective-permute-start(bf16[256,512]{1,0:T(8,128)(2,1)S(1)} %maximum_select_fusion.1.pieces_4_), channel_id=1, source_target_pairs={{0,1},{1,0},{4,5},{5,4},{8,9},{9,8},{12,13},{13,12},{16,17},{17,16... | collective-permute-start | bytes 786440 | tf_op jit(solution)/shard_map/ppermute | solution.py:262
  21.0 12.0 %copy-start.6 = (bf16[256,512]{1,0:T(8,128)(2,1)}, bf16[256,512]{1,0:T(8,128)(2,1)S(1)}, u32[]{:S(2)}) copy-start(bf16[256,512]{1,0:T(8,128)(2,1)S(1)} %collective-permute-done.5.pieces_2_) | copy-start | bytes 786436
  21.0 7.9 %collective-permute-start.6 = (bf16[256,512]{1,0:T(8,128)(2,1)S(1)}, bf16[256,512]{1,0:T(8,128)(2,1)S(1)}, u32[]{:S(2)}, u32[]{:S(2)}) collective-permute-start(bf16[256,512]{1,0:T(8,128)(2,1)S(1)} %collective-permute-done.5.pieces_2_), channel_id=1, source_target_pairs={{0,1},{1,0},{4,5},{5,4},{8,9},{9,8},{12,13},{13,12},{16,17},{17,16... | collective-permute-start | bytes 786440 | tf_op jit(solution)/shard_map/ppermute | solution.py:262
  23.8 9.1 %copy-start.7 = (bf16[256,512]{1,0:T(8,128)(2,1)}, bf16[256,512]{1,0:T(8,128)(2,1)S(1)}, u32[]{:S(2)}) copy-start(bf16[256,512]{1,0:T(8,128)(2,1)S(1)} %collective-permute-done.3.pieces_0_) | copy-start | bytes 786436
  23.9 9.1 %collective-permute-start.4 = (bf16[256,512]{1,0:T(8,128)(2,1)S(1)}, bf16[256,512]{1,0:T(8,128)(2,1)S(1)}, u32[]{:S(2)}, u32[]{:S(2)}) collective-permute-start(bf16[256,512]{1,0:T(8,128)(2,1)S(1)} %collective-permute-done.3.pieces_0_), channel_id=1, source_target_pairs={{0,1},{1,0},{4,5},{5,4},{8,9},{9,8},{12,13},{13,12},{16,17},{17,16... | collective-permute-start | bytes 786440 | tf_op jit(solution)/shard_map/ppermute | solution.py:262
  24.0 9.0 %copy-start.8 = (bf16[256,512]{1,0:T(8,128)(2,1)}, bf16[256,512]{1,0:T(8,128)(2,1)S(1)}, u32[]{:S(2)}) copy-start(bf16[256,512]{1,0:T(8,128)(2,1)S(1)} %collective-permute-done.7.pieces_5_) | copy-start | bytes 786436
  24.0 9.0 %copy-start.3 = (bf16[128,2048]{1,0:T(8,128)(2,1)}, bf16[128,2048]{1,0:T(8,128)(2,1)S(1)}, u32[]{:S(2)}) copy-start(bf16[128,2048]{1,0:T(8,128)(2,1)S(1)} %collective-permute-done.1.g_got_ref) | copy-start | bytes 1572868
  24.0 9.0 %copy-start.4 = (bf16[128,2048]{1,0:T(8,128)(2,1)}, bf16[128,2048]{1,0:T(8,128)(2,1)S(1)}, u32[]{:S(2)}) copy-start(bf16[128,2048]{1,0:T(8,128)(2,1)S(1)} %collective-permute-done.q_got_ref) | copy-start | bytes 1572868
  28.9 4.1 %copy-start.9 = (bf16[256,512]{1,0:T(8,128)(2,1)}, bf16[256,512]{1,0:T(8,128)(2,1)S(1)}, u32[]{:S(2)}) copy-start(bf16[256,512]{1,0:T(8,128)(2,1)S(1)} %collective-permute-done.6.pieces_3_) | copy-start | bytes 786436
  33.0 0.7 copy-start.10
  56.4 18.6 %copy-start.13 = (bf16[128,2048]{1,0:T(8,128)(2,1)S(1)}, bf16[128,2048]{1,0:T(8,128)(2,1)}, u32[]{:S(2)}) copy-start(bf16[128,2048]{1,0:T(8,128)(2,1)} %get-tuple-element.18) | copy-start | bytes 1572868
  56.4 28.1 %copy-start.5 = (bf16[256,512]{1,0:T(8,128)(2,1)S(1)}, bf16[256,512]{1,0:T(8,128)(2,1)}, u32[]{:S(2)}) copy-start(bf16[256,512]{1,0:T(8,128)(2,1)} %get-tuple-element.23) | copy-start | bytes 786436
  56.4 9.5 %collective-permute-start.9 = (bf16[256,512]{1,0:T(8,128)(2,1)}, bf16[256,512]{1,0:T(8,128)(2,1)S(1)}, u32[]{:S(2)}, u32[]{:S(2)}) collective-permute-start(bf16[256,512]{1,0:T(8,128)(2,1)} %get-tuple-element.20), channel_id=1, source_target_pairs={{0,1},{1,0},{4,5},{5,4},{8,9},{9,8},{12,13},{13,12},{16,17},{17,16... | collective-permute-start | bytes 786440 | tf_op jit(solution)/shard_map/ppermute | solution.py:262
  58.1 13.5 %collective-permute-start.11 = (bf16[256,512]{1,0:T(8,128)(2,1)}, bf16[256,512]{1,0:T(8,128)(2,1)S(1)}, u32[]{:S(2)}, u32[]{:S(2)}) collective-permute-start(bf16[256,512]{1,0:T(8,128)(2,1)} %get-tuple-element.22), channel_id=1, source_target_pairs={{0,1},{1,0},{4,5},{5,4},{8,9},{9,8},{12,13},{13,12},{16,17},{17,16... | collective-permute-start | bytes 786440 | tf_op jit(solution)/shard_map/ppermute | solution.py:262
  58.5 16.8 %collective-permute-start.13 = (bf16[256,512]{1,0:T(8,128)(2,1)}, bf16[256,512]{1,0:T(8,128)(2,1)S(1)}, u32[]{:S(2)}, u32[]{:S(2)}) collective-permute-start(bf16[256,512]{1,0:T(8,128)(2,1)} %get-tuple-element.24), channel_id=1, source_target_pairs={{0,1},{1,0},{4,5},{5,4},{8,9},{9,8},{12,13},{13,12},{16,17},{17,16... | collective-permute-start | bytes 786440 | tf_op jit(solution)/shard_map/ppermute | solution.py:262
  67.0 15.8 %collective-permute-start.10 = (bf16[256,512]{1,0:T(8,128)(2,1)S(1)}, bf16[256,512]{1,0:T(8,128)(2,1)S(1)}, u32[]{:S(2)}, u32[]{:S(2)}) collective-permute-start(bf16[256,512]{1,0:T(8,128)(2,1)S(1)} %add_convert_fusion.2), channel_id=1, source_target_pairs={{16,0},{17,1},{20,4},{21,5},{24,8},{25,9},{28,12},{29,13},{32,16},... | collective-permute-start | bytes 786440 | tf_op jit(solution)/shard_map/ppermute | solution.py:262
  72.6 12.7 %copy-start.2 = (bf16[128,2048]{1,0:T(8,128)(2,1)S(1)}, bf16[128,2048]{1,0:T(8,128)(2,1)}, u32[]{:S(2)}) copy-start(bf16[128,2048]{1,0:T(8,128)(2,1)} %get-tuple-element.17) | copy-start | bytes 1572868
  72.6 11.9 %collective-permute-start.12 = (bf16[256,512]{1,0:T(8,128)(2,1)S(1)}, bf16[256,512]{1,0:T(8,128)(2,1)S(1)}, u32[]{:S(2)}, u32[]{:S(2)}) collective-permute-start(bf16[256,512]{1,0:T(8,128)(2,1)S(1)} %add_convert_fusion.1), channel_id=1, source_target_pairs={{8,0},{9,1},{12,4},{13,5},{16,8},{17,9},{20,12},{21,13},{24,16},{2... | collective-permute-start | bytes 786440 | tf_op jit(solution)/shard_map/ppermute | solution.py:262
  75.0 10.3 %collective-permute-start.8 = (bf16[128,2048]{1,0:T(8,128)(2,1)S(1)}, bf16[128,2048]{1,0:T(8,128)(2,1)S(1)}, u32[]{:S(2)}, u32[]{:S(2)}) collective-permute-start(bf16[128,2048]{1,0:T(8,128)(2,1)S(1)} %copy-done.13), channel_id=1, source_target_pairs={{0,4},{1,5},{4,0},{5,1},{8,12},{9,13},{12,8},{13,9},{16,20},{17,21... | collective-permute-start | bytes 1572872 | tf_op jit(solution)/shard_map/ppermute | solution.py:262
  85.3 1.3 %collective-permute-start.14 = (bf16[128,512]{1,0:T(8,128)(2,1)S(1)}, bf16[128,512]{1,0:T(8,128)(2,1)S(1)}, u32[]{:S(2)}, u32[]{:S(2)}) collective-permute-start(bf16[128,512]{1,0:T(8,128)(2,1)S(1)} %get-tuple-element.27), channel_id=1, source_target_pairs={{0,4},{1,5},{4,0},{5,1},{8,12},{9,13},{12,8},{13,9},{16,20},{17,21... | collective-permute-start | bytes 393224 | tf_op jit(solution)/shard_map/ppermute | solution.py:262
  86.6 0.7 copy-start.12

commit v2 on v1

v2 whole, which is shorter than its diff:
```python
import math

import jax
import jax.numpy as jnp
from jax import lax
from jax.experimental import pallas as pl
from jax.experimental.pallas import tpu as pltpu
from jax.sharding import PartitionSpec as P

HD = 128
AXES = ("ctx", "kv")
BACK = 8
TILE = 3
NEG = -1e30
NT = (((1,), (1,)), ((), ()))
SCALE = 1.0 / math.sqrt(HD)
SCALE_LOG2 = math.log2(math.e) / math.sqrt(HD)


def device_of(n_ctx, group, core, part):
    if group < n_ctx // 2:
        return (2 * group + core) * 4 + part
    return (2 * (n_ctx - 1 - group) + core) * 4 + part + 2


def pairs(n_ctx, move):
    found = []
    for group in range(n_ctx):
        for core in range(2):
            for part in range(2):
                target = move(group, core, part)
                if 0 <= target[0] < n_ctx:
                    found.append((device_of(n_ctx, group, core, part), device_of(n_ctx, *target)))
    return found


def ahead(n_ctx, steps):
    def move(group, core, part):
        crosses = (group < n_ctx // 2) != (group + steps < n_ctx // 2)
        return group + steps, core, part ^ int(crosses)

    return pairs(n_ctx, move)


def heads_of(ref, cols):
    return ref[:, pl.ds(pl.multiple_of(cols, HD), HD)]


def split_kernel(keys_ref, values_ref, mine_ref, send_ref):
    core = lax.axis_index("ctx") % 2
    kept = mine_ref.shape[1] // (2 * HD)
    for ref, side in ((mine_ref, core), (send_ref, 1 - core)):
        for a in range(kept):
            cols = (side * kept + a) * HD
            ref[:, 2 * a * HD : (2 * a + 1) * HD] = heads_of(keys_ref, cols)
            ref[:, (2 * a + 1) * HD : (2 * a + 2) * HD] = heads_of(values_ref, cols)


def merge_kernel(mine_ref, got_ref, key_ref, value_ref):
    core = lax.axis_index("ctx") % 2
    kept = mine_ref.shape[1] // (2 * HD)
    for ref, side in ((mine_ref, core), (got_ref, 1 - core)):
        for a in range(kept):
            cols = pl.ds(pl.multiple_of((side * kept + a) * HD, HD), HD)
            key_ref[:, cols] = ref[:, 2 * a * HD : (2 * a + 1) * HD]
            value_ref[:, cols] = ref[:, (2 * a + 1) * HD : (2 * a + 2) * HD]


def kernel(
    lengths_ref, q_own_ref, q_got_ref, g_own_ref, g_got_ref, pieces, dq_mine_ref, dq_send_ref, parts,
    win, acc, key_acc, value_acc, s_scr, pp_scr, dp_scr, p_scr, ds_scr,
):
    q_refs, g_refs, dq_refs = (q_own_ref, q_got_ref), (g_own_ref, g_got_ref), (dq_mine_ref, dq_send_ref)
    rows, span = q_own_ref.shape
    pair_count = span // (2 * HD)
    width = (BACK + 1) * rows
    high = TILE * rows
    n_ctx = lax.axis_size("ctx")
    turn = n_ctx // 2
    slot = lax.axis_index("ctx")
    lane = lax.axis_index("kv")
    upper = lane // 2
    part = lane % 2
    core = slot % 2
    group = jnp.where(upper == 0, slot // 2, n_ctx - 1 - slot // 2)

    def spot(which, y_rel, core):
        crossed = jnp.where((group >= turn) & (group < turn + 2 - which), 1, 0)
        index = 4 * which + 2 * (core ^ upper ^ crossed) + (part ^ y_rel ^ crossed)
        return pl.ds(pl.multiple_of(index * rows, rows), rows)

    spots = [(which, y_rel, core) for which in range(3) for y_rel in range(2) for core in range(2)]
    for which, y_rel, side in spots:
        win[spot(which, y_rel, side), :] = pieces[2 * which + y_rel][side * rows : (side + 1) * rows, :]

    lens = lengths_ref[...].astype(jnp.float32)
    docs = lens.shape[1]
    below = lax.broadcasted_iota(jnp.int32, (docs, docs), 1) <= lax.broadcasted_iota(jnp.int32, (docs, docs), 0)
    ends = jnp.sum(jnp.where(below, lens, 0.0), axis=1, keepdims=True)
    column = lax.broadcasted_iota(jnp.int32, (1, 2 * rows), 1) % rows
    base, low, keys_t = [], [], []
    for other in range(2):
        first = 2 * (core ^ other ^ upper) + part
        start = (4 * group + first) * rows
        pos = (start + lax.broadcasted_iota(jnp.int32, (1, rows), 1)).astype(jnp.float32)
        lo = jnp.max(jnp.where(ends <= pos, ends, 0.0), axis=0, keepdims=True).astype(jnp.int32)
        lo = lo - (start - BACK * rows)
        low.append(jnp.concatenate([lo, lo], axis=1))
        base.append(first * rows)
        keys_t.append(win[pl.ds(pl.multiple_of(first * rows, rows), width), :HD].T)

    units = [(other, pair) for other in range(2) for pair in range(pair_count)]
    tiles = range((BACK + 1) // TILE)
    state = {}

    def key_rows(unit, t):
        return pl.ds(pl.multiple_of(base[units[unit][0]] + t * high, rows), high)

    def lanes(unit):
        return slice(unit * 2 * rows, (unit + 1) * 2 * rows)

    def pair_of(refs, unit):
        other, pair = units[unit]
        return jnp.concatenate(
            [refs[other][:, (2 * pair + i) * HD : (2 * pair + i + 1) * HD] for i in range(2)], axis=0
        )

    def folded(tile, fold):
        return fold(tile.reshape(high // 8, 8, 2 * rows), axis=0)

    def scores(unit):
        slot = unit % 4
        for t in tiles:
            tile = lax.dot_general(
                win[key_rows(unit, t), :HD], pair_of(q_refs, unit), NT, preferred_element_type=jnp.float32
            )
            key_row = lax.broadcasted_iota(jnp.int32, (high, 2 * rows), 0) + t * high
            allowed = key_row >= low[units[unit][0]]
            if t == tiles[-1]:
                allowed = allowed & (key_row - BACK * rows <= column)
            tile = jnp.where(allowed, tile, NEG)
            s_scr[slot, t * high : (t + 1) * high, :] = tile
            peak = folded(tile, jnp.max)
            state["top", unit] = peak if t == 0 else jnp.maximum(state["top", unit], peak)
        state["top", unit] = jnp.max(state["top", unit], axis=0, keepdims=True) * SCALE_LOG2
        state["total", unit] = state["dots", unit] = jnp.zeros((8, 2 * rows), jnp.float32)

    def weight_tile(unit, t):
        here = slice(t * high, (t + 1) * high)
        weight = jnp.exp2(s_scr[unit % 4, here, :] * SCALE_LOG2 - state["top", unit])
        grad_prob = lax.dot_general(
            win[key_rows(unit, t), HD:], pair_of(g_refs, unit), NT, preferred_element_type=jnp.float32
        )
        pp_scr[unit % 4, here, :] = weight
        dp_scr[unit % 4, here, :] = grad_prob
        state["total", unit] += folded(weight, jnp.sum)
        state["dots", unit] += folded(weight * grad_prob, jnp.sum)

    def sums(unit):
        state["inverse", unit] = 1.0 / jnp.sum(state["total", unit], axis=0, keepdims=True)
        state["delta", unit] = jnp.sum(state["dots", unit], axis=0, keepdims=True) * state["inverse", unit]

    def prob_tile(unit, t):
        here = slice(t * high, (t + 1) * high)
        prob = pp_scr[unit % 4, here, :] * state["inverse", unit]
        p_scr[here, lanes(unit % 4)] = prob.astype(jnp.bfloat16)
        ds_scr[here, lanes(unit % 4)] = (prob * (dp_scr[unit % 4, here, :] - state["delta", unit])).astype(
            jnp.bfloat16
        )

    def products(unit):
        other, pair = units[unit]
        dscore, prob = ds_scr[:, lanes(unit % 4)], p_scr[:, lanes(unit % 4)]
        dq = jnp.dot(keys_t[other], dscore, preferred_element_type=jnp.float32).T * SCALE
        dq = dq.astype(jnp.bfloat16)
        dq_refs[other][:, 2 * pair * HD : (2 * pair + 1) * HD] = dq[:rows]
        dq_refs[other][:, (2 * pair + 1) * HD : (2 * pair + 2) * HD] = dq[rows:]
        key_part = jnp.dot(dscore, pair_of(q_refs, unit), preferred_element_type=jnp.float32)
        value_part = jnp.dot(prob, pair_of(g_refs, unit), preferred_element_type=jnp.float32)
        if pair == 0:
            key_acc[other] = key_part
            value_acc[other] = value_part
        else:
            key_acc[other] += key_part
            value_acc[other] += value_part

    scores(0)
    for t in tiles:
        weight_tile(0, t)
    sums(0)
    scores(1)
    for unit in range(len(units)):
        for t in tiles:
            prob_tile(unit, t)
            if unit + 1 < len(units):
                weight_tile(unit + 1, t)
        if unit + 1 < len(units):
            sums(unit + 1)
        if unit + 2 < len(units):
            scores(unit + 2)
        products(unit)

    acc[...] = jnp.zeros_like(acc)
    for other in range(2):
        here = pl.ds(pl.multiple_of(base[other], rows), width)
        acc[here, :HD] += key_acc[other] * SCALE
        acc[here, HD:] += value_acc[other]
    for which, y_rel, side in spots:
        parts[2 * which + y_rel][side * rows : (side + 1) * rows, :] = acc[spot(which, y_rel, side), :].astype(
            jnp.bfloat16
        )


def attention(lengths, queries, q_got, grad_out, g_got, pieces):
    rows, q_width = q_got.shape
    kv_heads = pieces[0].shape[1] // (2 * HD)
    span = q_width // kv_heads
    heads = span // HD
    width = (BACK + 1) * rows
    by_core = pl.BlockSpec((rows, span), lambda a: (0, kv_heads * (lax.axis_index("ctx") % 2) + a))
    by_head = pl.BlockSpec((rows, span), lambda a: (0, a))
    piece = pl.BlockSpec((2 * rows, 2 * HD), lambda a: (0, a))
    tile = pltpu.VMEM((heads // 2, width, 2 * rows), jnp.float32)
    flat = pltpu.VMEM((width, heads * rows), jnp.bfloat16)
    half = jax.ShapeDtypeStruct((rows, q_width), jnp.bfloat16)
    return pl.pallas_call(
        kernel,
        grid=(kv_heads,),
        in_specs=[
            pl.BlockSpec(lengths.shape, lambda a: (0, 0)),
            by_core,
            by_head,
            by_core,
            by_head,
            [piece] * 6,
        ],
        out_specs=[by_head, by_head, [piece] * 6],
        out_shape=[half, half, [jax.ShapeDtypeStruct(pieces[0].shape, jnp.bfloat16)] * 6],
        scratch_shapes=[
            pltpu.VMEM((12 * rows, 2 * HD), jnp.bfloat16),
            pltpu.VMEM((12 * rows, 2 * HD), jnp.float32),
            pltpu.VMEM((2, width, HD), jnp.float32),
            pltpu.VMEM((2, width, HD), jnp.float32),
            tile,
            tile,
            tile,
            flat,
            flat,
        ],
        compiler_params=pltpu.CompilerParams(vmem_limit_bytes=56 * 2**20),
    )(lengths, queries, q_got, grad_out, g_got, pieces)


def body(queries, keys, values, grad_out, doc_lengths):
    n_ctx = lax.axis_size("ctx")
    core = lax.axis_index("ctx") % 2
    swap_part = pairs(n_ctx, lambda g, c, y: (g, c, 1 - y))
    swap_core = pairs(n_ctx, lambda g, c, y: (g, 1 - c, y))
    rows, kv_width = keys.shape

    def sent(value, plan):
        return lax.ppermute(value, AXES, plan)

    def other_heads(value):
        half = value.shape[1] // 2
        return sent(lax.dynamic_slice_in_dim(value, (1 - core) * half, half, 1), swap_core)

    def in_order(mine, got, axis):
        return jnp.where(
            core == 0, jnp.concatenate([mine, got], axis=axis), jnp.concatenate([got, mine], axis=axis)
        )

    def added(*terms):
        return sum(term.astype(jnp.float32) for term in terms)

    chunk = jax.ShapeDtypeStruct(keys.shape, jnp.bfloat16)
    mine, given = pl.pallas_call(split_kernel, out_shape=[chunk, chunk])(keys, values)
    own = in_order(mine, sent(given, swap_core), 0)
    far, near, beside = sent(own, ahead(n_ctx, 2)), sent(own, ahead(n_ctx, 1)), sent(own, swap_part)
    near, beside = lax.optimization_barrier((near, beside))
    pieces = [far, sent(far, swap_part), near, sent(near, swap_part), own, beside]
    dq_mine, dq_send, parts = attention(
        doc_lengths.reshape(1, -1), queries, other_heads(queries), grad_out, other_heads(grad_out), pieces
    )
    query_grad = in_order(dq_mine, sent(dq_send, swap_core), 1)
    total = None
    for which in range(3):
        summed = added(parts[2 * which], sent(parts[2 * which + 1], swap_part))
        if which < 2:
            summed = sent(summed.astype(jnp.bfloat16), ahead(n_ctx, which - 2))
            summed = summed.astype(jnp.float32)
        total = summed if total is None else total + summed
    total = total.astype(jnp.bfloat16)
    given = lax.dynamic_slice_in_dim(total, (1 - core) * rows, rows, 0)
    mine = lax.dynamic_slice_in_dim(total, core * rows, rows, 0)
    key_grad, value_grad = pl.pallas_call(merge_kernel, out_shape=[chunk, chunk])(mine, sent(given, swap_core))
    return query_grad, key_grad, value_grad


def solution(mesh):
    rows = P(AXES, None)
    return jax.shard_map(
        body,
        mesh=mesh,
        in_specs=(rows, rows, rows, rows, P()),
        out_specs=(rows, rows, rows),
        check_vma=False,
    )
```

time: 90.3 us -> 86.7 us (0.960)
  Pallas kernels: 26.2 us -> 23.1 us
  starting transfers between devices: 19.9 us -> 16.8 us
  waiting for transfers between devices: 35.4 us -> 37.9 us
    pallas_call x1, Pallas kernels: 22.7 us -> 19.6 us  [attention(): pl.pallas_call(kernel, grid=(kv_heads,), in_specs=[pl.BlockSpec(lengths.s...]
    ppermute x15, starting transfers between devices: 19.9 us -> 16.8 us  [sent(): return lax.ppermute(value, AXES, plan)]
    ppermute x15, waiting for transfers between devices: 35.4 us -> 37.9 us  [sent(): return lax.ppermute(value, AXES, plan)]
  transfers between devices with their start and end apart: 15 -> 15, of which waited for: 10 -> 9; matrix products, arithmetic and copies ran while one was open for 6% -> 6% of each run, Pallas kernels for 0% -> 0%
where the time goes in v2:
time: 86.7 us; the launch traced here: 85.4 us
  waiting for transfers between devices  37.9 us (44%)
  Pallas kernels  23.1 us (27%)
  starting transfers between devices  16.8 us (19%)
  other arithmetic  3.44 us (4%)
  local copies, waits for them, and re-layouts  3.2 us (4%)
  between operations  0.87 us (1%)
    ppermute x15, waiting for transfers between devices, sent(): return lax.ppermute(value, AXES, plan)  37.9 us
    pallas_call x1, Pallas kernels, attention(): pl.pallas_call(kernel, grid=(kv_heads,), in_specs=[pl.BlockSpec(lengths.s...  19.6 us
    ppermute x15, starting transfers between devices, sent(): return lax.ppermute(value, AXES, plan)  16.8 us
    convert_element_type x2, other arithmetic, body(): summed = sent(summed.astype(jnp.bfloat16), ahead(n_ctx, which - 2))  2.03 us
    pallas_call x1, Pallas kernels, body(): pl.pallas_call(split_kernel, out_shape=[chunk, chunk])(keys, values)  1.8 us
  transfers between devices with their start and end apart: 15, of which 9 were waited for; matrix products, arithmetic and copies ran while one was open for 6% of the time, Pallas kernels for 0%

profile of v2, /device:TPU:230, one launch (start us, length us, event | category | flops | bytes accessed | tf_op | source)
XLA Modules:
  0.0 85.4 jit_solution(11539191452078682310)
XLA Ops:
  0.6 0.0 copy-start
  0.6 1.8 %shard_map.76 = (bf16[128,512]{1,0:T(8,128)(2,1)}, bf16[128,512]{1,0:T(8,128)(2,1)}) custom-call(bf16[128,512]{1,0:T(8,128)(2,1)} %keys_ref.1, bf16[128,512]{1,0:T(8,128)(2,1)} %values_ref.1), custom_call_target="tpu_custom_call" | custom-call | tf_op jit(solution)/shard_map/pallas_call | solution.py:277
  2.4 0.0 copy-start.11
  2.4 0.0 collective-permute-start.2
  2.4 1.1 %constant_dynamic-slice_fusion.2 = bf16[128,2048]{1,0:T(8,128)(2,1)S(1)} fusion(bf16[128,4096]{1,0:T(8,128)(2,1)} %g_own_ref.1, s32[]{:T(128)S(6)} %select_n.35), kind=kLoop, calls=%fused_computation.7 | loop fusion | bytes 1048580 | tf_op jit(solution)/shard_map/dynamic_slice | solution.py:266
  3.6 0.6 collective-permute-start.1
  4.1 0.0 collective-permute-done.2
  4.1 0.0 copy-done.11
  4.1 0.1 maximum_select_fusion.1.pieces_4_
  4.2 0.0 copy-start.1
  4.2 1.7 %collective-permute-start.6 = (bf16[256,512]{1,0:T(8,128)(2,1)S(1)}, bf16[256,512]{1,0:T(8,128)(2,1)S(1)}, u32[]{:S(2)}, u32[]{:S(2)}) collective-permute-start(bf16[256,512]{1,0:T(8,128)(2,1)S(1)} %maximum_select_fusion.1.pieces_4_), channel_id=1, source_target_pairs={{0,1},{1,0},{4,5},{5,4},{8,9},{9,8},{12,13},{13,12},{16,17},{17,16... | collective-permute-start | bytes 786440 | tf_op jit(solution)/shard_map/ppermute | solution.py:262
  5.9 4.1 %collective-permute-start.5 = (bf16[256,512]{1,0:T(8,128)(2,1)S(1)}, bf16[256,512]{1,0:T(8,128)(2,1)S(1)}, u32[]{:S(2)}, u32[]{:S(2)}) collective-permute-start(bf16[256,512]{1,0:T(8,128)(2,1)S(1)} %maximum_select_fusion.1.pieces_4_), channel_id=1, source_target_pairs={{0,8},{1,9},{4,12},{5,13},{8,16},{9,17},{12,20},{13,21},{16,24},{1... | collective-permute-start | bytes 786440 | tf_op jit(solution)/shard_map/ppermute | solution.py:262
  9.9 0.0 copy-done
  10.0 0.1 collective-permute-start
  10.1 2.7 %collective-permute-start.3 = (bf16[256,512]{1,0:T(8,128)(2,1)S(1)}, bf16[256,512]{1,0:T(8,128)(2,1)S(1)}, u32[]{:S(2)}, u32[]{:S(2)}) collective-permute-start(bf16[256,512]{1,0:T(8,128)(2,1)S(1)} %maximum_select_fusion.1.pieces_4_), channel_id=1, source_target_pairs={{0,16},{1,17},{4,20},{5,21},{8,24},{9,25},{12,28},{13,29},{16,32},... | collective-permute-start | bytes 786440 | tf_op jit(solution)/shard_map/ppermute | solution.py:262
  12.8 0.0 collective-permute-done.6.pieces_5_
  12.8 0.0 copy-start.6
  12.8 9.4 %collective-permute-done.5.pieces_2_ = bf16[256,512]{1,0:T(8,128)(2,1)S(1)} collective-permute-done((bf16[256,512]{1,0:T(8,128)(2,1)S(1)}, bf16[256,512]{1,0:T(8,128)(2,1)S(1)}, u32[]{:S(2)}, u32[]{:S(2)}) %collective-permute-start.5) | collective-permute-done | bytes 262176 | tf_op jit(solution)/shard_map/ppermute | solution.py:262
  22.3 0.0 copy-start.7
  22.3 0.4 collective-permute-start.7
  22.7 1.9 %collective-permute-done.3.pieces_0_ = bf16[256,512]{1,0:T(8,128)(2,1)S(1)} collective-permute-done((bf16[256,512]{1,0:T(8,128)(2,1)S(1)}, bf16[256,512]{1,0:T(8,128)(2,1)S(1)}, u32[]{:S(2)}, u32[]{:S(2)}) %collective-permute-start.3) | collective-permute-done | bytes 262176 | tf_op jit(solution)/shard_map/ppermute | solution.py:262
  24.6 0.0 copy-start.8
  24.6 0.7 collective-permute-start.4
  25.3 0.0 collective-permute-done.1.g_got_ref
  25.3 0.0 collective-permute-done.q_got_ref
  25.3 0.0 copy-start.4
  25.3 5.0 %collective-permute-done.7.pieces_3_ = bf16[256,512]{1,0:T(8,128)(2,1)S(1)} collective-permute-done((bf16[256,512]{1,0:T(8,128)(2,1)S(1)}, bf16[256,512]{1,0:T(8,128)(2,1)S(1)}, u32[]{:S(2)}, u32[]{:S(2)}) %collective-permute-start.7) | collective-permute-done | bytes 262176 | tf_op jit(solution)/shard_map/ppermute | solution.py:262
  30.4 3.9 %collective-permute-done.4.pieces_1_ = bf16[256,512]{1,0:T(8,128)(2,1)S(1)} collective-permute-done((bf16[256,512]{1,0:T(8,128)(2,1)S(1)}, bf16[256,512]{1,0:T(8,128)(2,1)S(1)}, u32[]{:S(2)}, u32[]{:S(2)}) %collective-permute-start.4) | collective-permute-done | bytes 262176 | tf_op jit(solution)/shard_map/ppermute | solution.py:262
  34.3 0.0 copy-done.1
  34.3 0.0 copy-done.6
  34.3 0.0 copy-done.7
  34.3 0.0 copy-done.8
  34.3 0.0 copy-done.3
  34.3 0.0 copy-done.4
  34.3 0.0 copy-done.9
  34.3 0.7 copy-done.10
  35.0 19.6 %shard_map.77 = (bf16[128,2048]{1,0:T(8,128)(2,1)}, bf16[128,2048]{1,0:T(8,128)(2,1)}, bf16[256,512]{1,0:T(8,128)(2,1)}, bf16[256,512]{1,0:T(8,128)(2,1)}, bf16[...) custom-call(s32[1,64]{1,0:T(1,128)} %bitcast.1, ...), custom_call_target="tpu_custom_call" | custom-call | tf_op jit(solution)/shard_map/pallas_call | solution.py:226
  54.6 0.0 copy-start.13
  54.6 0.0 copy-start.5
  54.6 0.5 collective-permute-start.9
  55.1 1.6 %collective-permute-start.11 = (bf16[256,512]{1,0:T(8,128)(2,1)}, bf16[256,512]{1,0:T(8,128)(2,1)S(1)}, u32[]{:S(2)}, u32[]{:S(2)}) collective-permute-start(bf16[256,512]{1,0:T(8,128)(2,1)} %get-tuple-element.26), channel_id=1, source_target_pairs={{0,1},{1,0},{4,5},{5,4},{8,9},{9,8},{12,13},{13,12},{16,17},{17,16... | collective-permute-start | bytes 786440 | tf_op jit(solution)/shard_map/ppermute | solution.py:262
  56.7 0.4 collective-permute-start.13
  57.2 7.0 %collective-permute-done.9 = bf16[256,512]{1,0:T(8,128)(2,1)S(1)} collective-permute-done((bf16[256,512]{1,0:T(8,128)(2,1)}, bf16[256,512]{1,0:T(8,128)(2,1)S(1)}, u32[]{:S(2)}, u32[]{:S(2)}) %collective-permute-start.9) | collective-permute-done | bytes 262176 | tf_op jit(solution)/shard_map/ppermute | solution.py:262
  64.2 1.0 %add_convert_fusion.2 = bf16[256,512]{1,0:T(8,128)(2,1)S(1)} fusion(bf16[256,512]{1,0:T(8,128)(2,1)S(1)} %collective-permute-done.9, bf16[256,512]{1,0:T(8,128)(2,1)} %get-tuple-element.23), kind=kLoop, calls=%fused_computation.3 | loop fusion | flops 524288 | bytes 786432 | tf_op jit(solution)/shard_map/convert_element_type | solution.py:290
  65.2 1.9 %collective-permute-start.10 = (bf16[256,512]{1,0:T(8,128)(2,1)S(1)}, bf16[256,512]{1,0:T(8,128)(2,1)S(1)}, u32[]{:S(2)}, u32[]{:S(2)}) collective-permute-start(bf16[256,512]{1,0:T(8,128)(2,1)S(1)} %add_convert_fusion.2), channel_id=1, source_target_pairs={{16,0},{17,1},{20,4},{21,5},{24,8},{25,9},{28,12},{29,13},{32,16},... | collective-permute-start | bytes 786440 | tf_op jit(solution)/shard_map/ppermute | solution.py:262
  67.1 2.7 %collective-permute-done.11 = bf16[256,512]{1,0:T(8,128)(2,1)S(1)} collective-permute-done((bf16[256,512]{1,0:T(8,128)(2,1)}, bf16[256,512]{1,0:T(8,128)(2,1)S(1)}, u32[]{:S(2)}, u32[]{:S(2)}) %collective-permute-start.11) | collective-permute-done | bytes 262176 | tf_op jit(solution)/shard_map/ppermute | solution.py:262
  69.8 1.0 %add_convert_fusion.1 = bf16[256,512]{1,0:T(8,128)(2,1)S(1)} fusion(bf16[256,512]{1,0:T(8,128)(2,1)S(1)} %collective-permute-done.11, bf16[256,512]{1,0:T(8,128)(2,1)} %get-tuple-element.25), kind=kLoop, calls=%fused_computation.2 | loop fusion | flops 524288 | bytes 786432 | tf_op jit(solution)/shard_map/convert_element_type | solution.py:290
  70.8 0.0 copy-start.2
  70.8 2.1 %collective-permute-start.12 = (bf16[256,512]{1,0:T(8,128)(2,1)S(1)}, bf16[256,512]{1,0:T(8,128)(2,1)S(1)}, u32[]{:S(2)}, u32[]{:S(2)}) collective-permute-start(bf16[256,512]{1,0:T(8,128)(2,1)S(1)} %add_convert_fusion.1), channel_id=1, source_target_pairs={{8,0},{9,1},{12,4},{13,5},{16,8},{17,9},{20,12},{21,13},{24,16},{2... | collective-permute-start | bytes 786440 | tf_op jit(solution)/shard_map/ppermute | solution.py:262
  72.9 0.0 copy-done.13
  72.9 0.1 collective-permute-start.8
  73.0 0.0 collective-permute-done.13
  73.0 5.1 %collective-permute-done.10 = bf16[256,512]{1,0:T(8,128)(2,1)S(1)} collective-permute-done((bf16[256,512]{1,0:T(8,128)(2,1)S(1)}, bf16[256,512]{1,0:T(8,128)(2,1)S(1)}, u32[]{:S(2)}, u32[]{:S(2)}) %collective-permute-start.10) | collective-permute-done | bytes 262176 | tf_op jit(solution)/shard_map/ppermute | solution.py:262
  78.2 2.7 %collective-permute-done.12 = bf16[256,512]{1,0:T(8,128)(2,1)S(1)} collective-permute-done((bf16[256,512]{1,0:T(8,128)(2,1)S(1)}, bf16[256,512]{1,0:T(8,128)(2,1)S(1)}, u32[]{:S(2)}, u32[]{:S(2)}) %collective-permute-start.12) | collective-permute-done | bytes 262176 | tf_op jit(solution)/shard_map/ppermute | solution.py:262
  80.8 0.0 copy-done.5
  80.8 0.1 add_convert_fusion
  81.0 0.7 constant_dynamic-slice_fusion
  81.7 0.0 collective-permute-start.14
  81.7 0.0 collective-permute-done.8
  81.7 0.0 copy-done.2
  81.7 1.2 %maximum_select_fusion = bf16[128,4096]{1,0:T(8,128)(2,1)} fusion(bf16[128,2048]{1,0:T(8,128)(2,1)S(1)} %collective-permute-done.8, bf16[128,2048]{1,0:T(8,128)(2,1)S(1)} %copy-done.2, pred[]{:T(512)S(6)} %eq.6), kind=kLoop, calls=%fused_computation | loop fusion | flops 4718592 | bytes 2097153 | tf_op jit(solution)/shard_map/jit(_where)/select_n | solution.py:269
  82.9 0.1 collective-permute-done.14.got_ref
  83.0 0.7 copy-done.12
  83.7 1.7 %shard_map.78 = (bf16[128,512]{1,0:T(8,128)(2,1)}, bf16[128,512]{1,0:T(8,128)(2,1)}) custom-call(bf16[128,512]{1,0:T(8,128)(2,1)} %get-tuple-element.32.mine_ref, bf16[128,512]{1,0:T(8,128)(2,1)} %copy-done.12), custom_call_target="tpu_custom_call" | custom-call | tf_op jit(solution)/shard_map/pallas_call | solution.py:296
  (5 shorter events, 0.1 us)
Async XLA Ops:
  0.6 9.3 %copy-start = (bf16[128,4096]{1,0:T(8,128)(2,1)S(1)}, bf16[128,4096]{1,0:T(8,128)(2,1)}, u32[]{:S(2)}) copy-start(bf16[128,4096]{1,0:T(8,128)(2,1)} %q_own_ref.1) | copy-start | bytes 3145732
  2.4 1.7 %copy-start.11 = (bf16[128,512]{1,0:T(8,128)(2,1)S(1)}, bf16[128,512]{1,0:T(8,128)(2,1)}, u32[]{:S(2)}) copy-start(bf16[128,512]{1,0:T(8,128)(2,1)} %get-tuple-element.17) | copy-start | bytes 393220
  2.4 1.7 %collective-permute-start.2 = (bf16[128,512]{1,0:T(8,128)(2,1)}, bf16[128,512]{1,0:T(8,128)(2,1)S(1)}, u32[]{:S(2)}, u32[]{:S(2)}) collective-permute-start(bf16[128,512]{1,0:T(8,128)(2,1)} %get-tuple-element.18), channel_id=1, source_target_pairs={{0,4},{1,5},{4,0},{5,1},{8,12},{9,13},{12,8},{13,9},{16,20},{17,21... | collective-permute-start | bytes 393224 | tf_op jit(solution)/shard_map/ppermute | solution.py:262
  3.6 21.8 %collective-permute-start.1 = (bf16[128,2048]{1,0:T(8,128)(2,1)S(1)}, bf16[128,2048]{1,0:T(8,128)(2,1)S(1)}, u32[]{:S(2)}, u32[]{:S(2)}) collective-permute-start(bf16[128,2048]{1,0:T(8,128)(2,1)S(1)} %constant_dynamic-slice_fusion.2), channel_id=1, source_target_pairs={{0,4},{1,5},{4,0},{5,1},{8,12},{9,13},{12,8},{13,9},{16,20},{17,21... | collective-permute-start | bytes 1572872 | tf_op jit(solution)/shard_map/ppermute | solution.py:262
  4.2 30.1 %copy-start.1 = (bf16[256,512]{1,0:T(8,128)(2,1)}, bf16[256,512]{1,0:T(8,128)(2,1)S(1)}, u32[]{:S(2)}) copy-start(bf16[256,512]{1,0:T(8,128)(2,1)S(1)} %maximum_select_fusion.1.pieces_4_) | copy-start | bytes 786436
  4.2 8.6 %collective-permute-start.6 = (bf16[256,512]{1,0:T(8,128)(2,1)S(1)}, bf16[256,512]{1,0:T(8,128)(2,1)S(1)}, u32[]{:S(2)}, u32[]{:S(2)}) collective-permute-start(bf16[256,512]{1,0:T(8,128)(2,1)S(1)} %maximum_select_fusion.1.pieces_4_), channel_id=1, source_target_pairs={{0,1},{1,0},{4,5},{5,4},{8,9},{9,8},{12,13},{13,12},{16,17},{17,16... | collective-permute-start | bytes 786440 | tf_op jit(solution)/shard_map/ppermute | solution.py:262
  5.9 16.4 %collective-permute-start.5 = (bf16[256,512]{1,0:T(8,128)(2,1)S(1)}, bf16[256,512]{1,0:T(8,128)(2,1)S(1)}, u32[]{:S(2)}, u32[]{:S(2)}) collective-permute-start(bf16[256,512]{1,0:T(8,128)(2,1)S(1)} %maximum_select_fusion.1.pieces_4_), channel_id=1, source_target_pairs={{0,8},{1,9},{4,12},{5,13},{8,16},{9,17},{12,20},{13,21},{16,24},{1... | collective-permute-start | bytes 786440 | tf_op jit(solution)/shard_map/ppermute | solution.py:262
  10.0 15.3 %collective-permute-start = (bf16[128,2048]{1,0:T(8,128)(2,1)S(1)}, bf16[128,2048]{1,0:T(8,128)(2,1)S(1)}, u32[]{:S(2)}, u32[]{:S(2)}) collective-permute-start(bf16[128,2048]{1,0:T(8,128)(2,1)S(1)} %constant_dynamic-slice_fusion.3), channel_id=1, source_target_pairs={{0,4},{1,5},{4,0},{5,1},{8,12},{9,13},{12,8},{13,9},{16,20},{17,21... | collective-permute-start | bytes 1572872 | tf_op jit(solution)/shard_map/ppermute | solution.py:262
  10.1 14.5 %collective-permute-start.3 = (bf16[256,512]{1,0:T(8,128)(2,1)S(1)}, bf16[256,512]{1,0:T(8,128)(2,1)S(1)}, u32[]{:S(2)}, u32[]{:S(2)}) collective-permute-start(bf16[256,512]{1,0:T(8,128)(2,1)S(1)} %maximum_select_fusion.1.pieces_4_), channel_id=1, source_target_pairs={{0,16},{1,17},{4,20},{5,21},{8,24},{9,25},{12,28},{13,29},{16,32},... | collective-permute-start | bytes 786440 | tf_op jit(solution)/shard_map/ppermute | solution.py:262
  12.8 21.4 %copy-start.6 = (bf16[256,512]{1,0:T(8,128)(2,1)}, bf16[256,512]{1,0:T(8,128)(2,1)S(1)}, u32[]{:S(2)}) copy-start(bf16[256,512]{1,0:T(8,128)(2,1)S(1)} %collective-permute-done.6.pieces_5_) | copy-start | bytes 786436
  22.3 12.0 %copy-start.7 = (bf16[256,512]{1,0:T(8,128)(2,1)}, bf16[256,512]{1,0:T(8,128)(2,1)S(1)}, u32[]{:S(2)}) copy-start(bf16[256,512]{1,0:T(8,128)(2,1)S(1)} %collective-permute-done.5.pieces_2_) | copy-start | bytes 786436
  22.3 8.1 %collective-permute-start.7 = (bf16[256,512]{1,0:T(8,128)(2,1)S(1)}, bf16[256,512]{1,0:T(8,128)(2,1)S(1)}, u32[]{:S(2)}, u32[]{:S(2)}) collective-permute-start(bf16[256,512]{1,0:T(8,128)(2,1)S(1)} %collective-permute-done.5.pieces_2_), channel_id=1, source_target_pairs={{0,1},{1,0},{4,5},{5,4},{8,9},{9,8},{12,13},{13,12},{16,17},{17,16... | collective-permute-start | bytes 786440 | tf_op jit(solution)/shard_map/ppermute | solution.py:262
  24.6 9.7 %copy-start.8 = (bf16[256,512]{1,0:T(8,128)(2,1)}, bf16[256,512]{1,0:T(8,128)(2,1)S(1)}, u32[]{:S(2)}) copy-start(bf16[256,512]{1,0:T(8,128)(2,1)S(1)} %collective-permute-done.3.pieces_0_) | copy-start | bytes 786436
  24.6 9.6 %collective-permute-start.4 = (bf16[256,512]{1,0:T(8,128)(2,1)S(1)}, bf16[256,512]{1,0:T(8,128)(2,1)S(1)}, u32[]{:S(2)}, u32[]{:S(2)}) collective-permute-start(bf16[256,512]{1,0:T(8,128)(2,1)S(1)} %collective-permute-done.3.pieces_0_), channel_id=1, source_target_pairs={{0,1},{1,0},{4,5},{5,4},{8,9},{9,8},{12,13},{13,12},{16,17},{17,16... | collective-permute-start | bytes 786440 | tf_op jit(solution)/shard_map/ppermute | solution.py:262
  25.3 9.0 %copy-start.3 = (bf16[128,2048]{1,0:T(8,128)(2,1)}, bf16[128,2048]{1,0:T(8,128)(2,1)S(1)}, u32[]{:S(2)}) copy-start(bf16[128,2048]{1,0:T(8,128)(2,1)S(1)} %collective-permute-done.1.g_got_ref) | copy-start | bytes 1572868
  25.3 9.0 %copy-start.4 = (bf16[128,2048]{1,0:T(8,128)(2,1)}, bf16[128,2048]{1,0:T(8,128)(2,1)S(1)}, u32[]{:S(2)}) copy-start(bf16[128,2048]{1,0:T(8,128)(2,1)S(1)} %collective-permute-done.q_got_ref) | copy-start | bytes 1572868
  30.4 4.0 %copy-start.9 = (bf16[256,512]{1,0:T(8,128)(2,1)}, bf16[256,512]{1,0:T(8,128)(2,1)S(1)}, u32[]{:S(2)}) copy-start(bf16[256,512]{1,0:T(8,128)(2,1)S(1)} %collective-permute-done.7.pieces_3_) | copy-start | bytes 786436
  34.3 0.7 copy-start.10
  54.6 18.3 %copy-start.13 = (bf16[128,2048]{1,0:T(8,128)(2,1)S(1)}, bf16[128,2048]{1,0:T(8,128)(2,1)}, u32[]{:S(2)}) copy-start(bf16[128,2048]{1,0:T(8,128)(2,1)} %get-tuple-element.22) | copy-start | bytes 1572868
  54.6 26.2 %copy-start.5 = (bf16[256,512]{1,0:T(8,128)(2,1)S(1)}, bf16[256,512]{1,0:T(8,128)(2,1)}, u32[]{:S(2)}) copy-start(bf16[256,512]{1,0:T(8,128)(2,1)} %get-tuple-element.27) | copy-start | bytes 786436
  54.6 9.5 %collective-permute-start.9 = (bf16[256,512]{1,0:T(8,128)(2,1)}, bf16[256,512]{1,0:T(8,128)(2,1)S(1)}, u32[]{:S(2)}, u32[]{:S(2)}) collective-permute-start(bf16[256,512]{1,0:T(8,128)(2,1)} %get-tuple-element.24), channel_id=1, source_target_pairs={{0,1},{1,0},{4,5},{5,4},{8,9},{9,8},{12,13},{13,12},{16,17},{17,16... | collective-permute-start | bytes 786440 | tf_op jit(solution)/shard_map/ppermute | solution.py:262
  55.1 14.7 %collective-permute-start.11 = (bf16[256,512]{1,0:T(8,128)(2,1)}, bf16[256,512]{1,0:T(8,128)(2,1)S(1)}, u32[]{:S(2)}, u32[]{:S(2)}) collective-permute-start(bf16[256,512]{1,0:T(8,128)(2,1)} %get-tuple-element.26), channel_id=1, source_target_pairs={{0,1},{1,0},{4,5},{5,4},{8,9},{9,8},{12,13},{13,12},{16,17},{17,16... | collective-permute-start | bytes 786440 | tf_op jit(solution)/shard_map/ppermute | solution.py:262
  56.7 16.3 %collective-permute-start.13 = (bf16[256,512]{1,0:T(8,128)(2,1)}, bf16[256,512]{1,0:T(8,128)(2,1)S(1)}, u32[]{:S(2)}, u32[]{:S(2)}) collective-permute-start(bf16[256,512]{1,0:T(8,128)(2,1)} %get-tuple-element.28), channel_id=1, source_target_pairs={{0,1},{1,0},{4,5},{5,4},{8,9},{9,8},{12,13},{13,12},{16,17},{17,16... | collective-permute-start | bytes 786440 | tf_op jit(solution)/shard_map/ppermute | solution.py:262
  65.2 13.0 %collective-permute-start.10 = (bf16[256,512]{1,0:T(8,128)(2,1)S(1)}, bf16[256,512]{1,0:T(8,128)(2,1)S(1)}, u32[]{:S(2)}, u32[]{:S(2)}) collective-permute-start(bf16[256,512]{1,0:T(8,128)(2,1)S(1)} %add_convert_fusion.2), channel_id=1, source_target_pairs={{16,0},{17,1},{20,4},{21,5},{24,8},{25,9},{28,12},{29,13},{32,16},... | collective-permute-start | bytes 786440 | tf_op jit(solution)/shard_map/ppermute | solution.py:262
  70.8 10.9 %copy-start.2 = (bf16[128,2048]{1,0:T(8,128)(2,1)S(1)}, bf16[128,2048]{1,0:T(8,128)(2,1)}, u32[]{:S(2)}) copy-start(bf16[128,2048]{1,0:T(8,128)(2,1)} %get-tuple-element.21) | copy-start | bytes 1572868
  70.8 10.0 %collective-permute-start.12 = (bf16[256,512]{1,0:T(8,128)(2,1)S(1)}, bf16[256,512]{1,0:T(8,128)(2,1)S(1)}, u32[]{:S(2)}, u32[]{:S(2)}) collective-permute-start(bf16[256,512]{1,0:T(8,128)(2,1)S(1)} %add_convert_fusion.1), channel_id=1, source_target_pairs={{8,0},{9,1},{12,4},{13,5},{16,8},{17,9},{20,12},{21,13},{24,16},{2... | collective-permute-start | bytes 786440 | tf_op jit(solution)/shard_map/ppermute | solution.py:262
  72.9 8.8 %collective-permute-start.8 = (bf16[128,2048]{1,0:T(8,128)(2,1)S(1)}, bf16[128,2048]{1,0:T(8,128)(2,1)S(1)}, u32[]{:S(2)}, u32[]{:S(2)}) collective-permute-start(bf16[128,2048]{1,0:T(8,128)(2,1)S(1)} %copy-done.13), channel_id=1, source_target_pairs={{0,4},{1,5},{4,0},{5,1},{8,12},{9,13},{12,8},{13,9},{16,20},{17,21... | collective-permute-start | bytes 1572872 | tf_op jit(solution)/shard_map/ppermute | solution.py:262
  81.7 1.3 %collective-permute-start.14 = (bf16[128,512]{1,0:T(8,128)(2,1)S(1)}, bf16[128,512]{1,0:T(8,128)(2,1)S(1)}, u32[]{:S(2)}, u32[]{:S(2)}) collective-permute-start(bf16[128,512]{1,0:T(8,128)(2,1)S(1)} %get-tuple-element.31), channel_id=1, source_target_pairs={{0,4},{1,5},{4,0},{5,1},{8,12},{9,13},{12,8},{13,9},{16,20},{17,21... | collective-permute-start | bytes 393224 | tf_op jit(solution)/shard_map/ppermute | solution.py:262
  83.0 0.7 copy-start.12

commit v3 on v2

--- a/solution.py
+++ b/solution.py
@@ -247,7 +247,7 @@
             flat,
             flat,
         ],
-        compiler_params=pltpu.CompilerParams(vmem_limit_bytes=56 * 2**20),
+        compiler_params=pltpu.CompilerParams(vmem_limit_bytes=36 * 2**20),
     )(lengths, queries, q_got, grad_out, g_got, pieces)
 
 
@@ -274,7 +274,8 @@
         return sum(term.astype(jnp.float32) for term in terms)
 
     chunk = jax.ShapeDtypeStruct(keys.shape, jnp.bfloat16)
-    mine, given = pl.pallas_call(split_kernel, out_shape=[chunk, chunk])(keys, values)
+    small = pltpu.CompilerParams(vmem_limit_bytes=4 * 2**20)
+    mine, given = pl.pallas_call(split_kernel, out_shape=[chunk, chunk], compiler_params=small)(keys, values)
     own = in_order(mine, sent(given, swap_core), 0)
     far, near, beside = sent(own, ahead(n_ctx, 2)), sent(own, ahead(n_ctx, 1)), sent(own, swap_part)
     near, beside = lax.optimization_barrier((near, beside))
@@ -293,7 +294,7 @@
     total = total.astype(jnp.bfloat16)
     given = lax.dynamic_slice_in_dim(total, (1 - core) * rows, rows, 0)
     mine = lax.dynamic_slice_in_dim(total, core * rows, rows, 0)
-    key_grad, value_grad = pl.pallas_call(merge_kernel, out_shape=[chunk, chunk])(mine, sent(given, swap_core))
+    key_grad, value_grad = pl.pallas_call(merge_kernel, out_shape=[chunk, chunk], compiler_params=small)(mine, sent(given, swap_core))
     return query_grad, key_grad, value_grad
 
 

time: 86.7 us -> 81.9 us (0.945)
  Pallas kernels: 23.1 us -> 19.2 us
  other arithmetic: 3.44 us -> 1.54 us
    pallas_call x2, Pallas kernels: 3.51 us -> 0.79 us  [the longest x1 0.75 us: body(): pl.pallas_call(merge_kernel, out_shape=[chunk, chunk], compiler_params=sm...]
    convert_element_type x2, other arithmetic: 2.03 us -> 0.13 us  [body(): summed = sent(summed.astype(jnp.bfloat16), ahead(n_ctx, which - 2))]
    pallas_call x1, Pallas kernels: 19.6 us -> 18.4 us  [attention(): pl.pallas_call(kernel, grid=(kv_heads,), in_specs=[pl.BlockSpec(lengths.s...]
    unnamed x28 -> x10, local copies, waits for them, and re-layouts: 1.37 us -> 1.9 us
  transfers between devices with their start and end apart: 15 -> 15, of which waited for: 9 -> 10; matrix products, arithmetic and copies ran while one was open for 6% -> 4% of each run, Pallas kernels for 0% -> 0%
where the time goes in v3:
time: 81.9 us; the launch traced here: 80.9 us
  waiting for transfers between devices  38.7 us (47%)
  Pallas kernels  19.2 us (23%)
  starting transfers between devices  16.7 us (20%)
  local copies, waits for them, and re-layouts  3.86 us (5%)
  other arithmetic  1.54 us (2%)
  between operations  0.82 us (1%)
    ppermute x15, waiting for transfers between devices, sent(): return lax.ppermute(value, AXES, plan)  38.7 us
    pallas_call x1, Pallas kernels, attention(): pl.pallas_call(kernel, grid=(kv_heads,), in_specs=[pl.BlockSpec(lengths.s...  18.4 us
    ppermute x15, starting transfers between devices, sent(): return lax.ppermute(value, AXES, plan)  16.7 us
    dynamic_slice x2, local copies, waits for them, and re-layouts, other_heads(): lax.dynamic_slice_in_dim(value, (1 - core) * half, half, 1)  1.93 us
    unnamed x10, local copies, waits for them, and re-layouts  1.9 us
  transfers between devices with their start and end apart: 15, of which 10 were waited for; matrix products, arithmetic and copies ran while one was open for 4% of the time, Pallas kernels for 0%

profile of v3, /device:TPU:230, one launch (start us, length us, event | category | flops | bytes accessed | tf_op | source)
XLA Modules:
  0.0 80.9 jit_solution(5266217426745293370)
XLA Ops:
  0.6 0.0 copy-start
  0.6 0.0 copy-start.2
  0.7 1.0 %copy-done.2 = bf16[128,512]{1,0:T(8,128)(2,1)S(1)} copy-done((bf16[128,512]{1,0:T(8,128)(2,1)S(1)}, bf16[128,512]{1,0:T(8,128)(2,1)}, u32[]{:S(2)}) %copy-start.2) | copy-done | bytes 131096
  1.6 0.0 copy-start.3
  1.6 0.9 %copy-done.3 = bf16[128,512]{1,0:T(8,128)(2,1)S(1)} copy-done((bf16[128,512]{1,0:T(8,128)(2,1)S(1)}, bf16[128,512]{1,0:T(8,128)(2,1)}, u32[]{:S(2)}) %copy-start.3) | copy-done | bytes 131096
  2.6 0.1 collective-permute-start.2
  2.7 1.9 %constant_dynamic-slice_fusion.2 = bf16[128,2048]{1,0:T(8,128)(2,1)} fusion(bf16[128,4096]{1,0:T(8,128)(2,1)} %g_own_ref.1, s32[]{:T(128)S(6)} %select_n.35), kind=kLoop, calls=%fused_computation.7 | loop fusion | bytes 1048580 | tf_op jit(solution)/shard_map/dynamic_slice | solution.py:266
  4.6 0.0 copy-start.1
  4.6 0.0 copy-start.4
  4.6 0.5 collective-permute-start.1
  5.1 0.0 collective-permute-done.2
  5.1 0.1 maximum_select_fusion.1.pieces_4_
  5.1 1.7 %collective-permute-start.6 = (bf16[256,512]{1,0:T(8,128)(2,1)S(1)}, bf16[256,512]{1,0:T(8,128)(2,1)S(1)}, u32[]{:S(2)}, u32[]{:S(2)}) collective-permute-start(bf16[256,512]{1,0:T(8,128)(2,1)S(1)} %maximum_select_fusion.1.pieces_4_), channel_id=1, source_target_pairs={{0,1},{1,0},{4,5},{5,4},{8,9},{9,8},{12,13},{13,12},{16,17},{17,16... | collective-permute-start | bytes 786440 | tf_op jit(solution)/shard_map/ppermute | solution.py:262
  6.8 4.1 %collective-permute-start.5 = (bf16[256,512]{1,0:T(8,128)(2,1)S(1)}, bf16[256,512]{1,0:T(8,128)(2,1)S(1)}, u32[]{:S(2)}, u32[]{:S(2)}) collective-permute-start(bf16[256,512]{1,0:T(8,128)(2,1)S(1)} %maximum_select_fusion.1.pieces_4_), channel_id=1, source_target_pairs={{0,8},{1,9},{4,12},{5,13},{8,16},{9,17},{12,20},{13,21},{16,24},{1... | collective-permute-start | bytes 786440 | tf_op jit(solution)/shard_map/ppermute | solution.py:262
  10.9 0.0 copy-done
  10.9 0.1 collective-permute-start
  11.0 2.7 %collective-permute-start.3 = (bf16[256,512]{1,0:T(8,128)(2,1)S(1)}, bf16[256,512]{1,0:T(8,128)(2,1)S(1)}, u32[]{:S(2)}, u32[]{:S(2)}) collective-permute-start(bf16[256,512]{1,0:T(8,128)(2,1)S(1)} %maximum_select_fusion.1.pieces_4_), channel_id=1, source_target_pairs={{0,16},{1,17},{4,20},{5,21},{8,24},{9,25},{12,28},{13,29},{16,32},... | collective-permute-start | bytes 786440 | tf_op jit(solution)/shard_map/ppermute | solution.py:262
  13.8 0.0 collective-permute-done.6.pieces_5_
  13.8 9.4 %collective-permute-done.5.pieces_2_ = bf16[256,512]{1,0:T(8,128)(2,1)S(1)} collective-permute-done((bf16[256,512]{1,0:T(8,128)(2,1)S(1)}, bf16[256,512]{1,0:T(8,128)(2,1)S(1)}, u32[]{:S(2)}, u32[]{:S(2)}) %collective-permute-start.5) | collective-permute-done | bytes 262176 | tf_op jit(solution)/shard_map/ppermute | solution.py:262
  23.2 0.4 collective-permute-start.7
  23.7 1.9 %collective-permute-done.3.pieces_0_ = bf16[256,512]{1,0:T(8,128)(2,1)S(1)} collective-permute-done((bf16[256,512]{1,0:T(8,128)(2,1)S(1)}, bf16[256,512]{1,0:T(8,128)(2,1)S(1)}, u32[]{:S(2)}, u32[]{:S(2)}) %collective-permute-start.3) | collective-permute-done | bytes 262176 | tf_op jit(solution)/shard_map/ppermute | solution.py:262
  25.6 0.7 collective-permute-start.4
  26.3 0.0 collective-permute-done.1.g_got_ref
  26.3 0.0 collective-permute-done.q_got_ref
  26.3 5.0 %collective-permute-done.7.pieces_3_ = bf16[256,512]{1,0:T(8,128)(2,1)S(1)} collective-permute-done((bf16[256,512]{1,0:T(8,128)(2,1)S(1)}, bf16[256,512]{1,0:T(8,128)(2,1)S(1)}, u32[]{:S(2)}, u32[]{:S(2)}) %collective-permute-start.7) | collective-permute-done | bytes 262176 | tf_op jit(solution)/shard_map/ppermute | solution.py:262
  31.3 3.9 %collective-permute-done.4.pieces_1_ = bf16[256,512]{1,0:T(8,128)(2,1)S(1)} collective-permute-done((bf16[256,512]{1,0:T(8,128)(2,1)S(1)}, bf16[256,512]{1,0:T(8,128)(2,1)S(1)}, u32[]{:S(2)}, u32[]{:S(2)}) %collective-permute-start.4) | collective-permute-done | bytes 262176 | tf_op jit(solution)/shard_map/ppermute | solution.py:262
  35.2 0.0 copy-done.1
  35.2 0.0 copy-done.4
  35.2 18.4 %shard_map.77 = (bf16[128,2048]{1,0:T(8,128)(2,1)S(1)}, bf16[128,2048]{1,0:T(8,128)(2,1)}, bf16[256,512]{1,0:T(8,128)(2,1)S(1)}, bf16[256,512]{1,0:T(8,128)(2,1)...) custom-call(s32[1,64]{1,0:T(1,128)S(1)} %bitcast.1, ...), custom_call_target="tpu_custom_call" | custom-call | tf_op jit(solution)/shard_map/pallas_call | solution.py:226
  53.7 0.4 collective-permute-start.9
  54.1 1.6 %collective-permute-start.11 = (bf16[256,512]{1,0:T(8,128)(2,1)S(1)}, bf16[256,512]{1,0:T(8,128)(2,1)S(1)}, u32[]{:S(2)}, u32[]{:S(2)}) collective-permute-start(bf16[256,512]{1,0:T(8,128)(2,1)S(1)} %get-tuple-element.26), channel_id=1, source_target_pairs={{0,1},{1,0},{4,5},{5,4},{8,9},{9,8},{12,13},{13,12},{16,17},{17,16... | collective-permute-start | bytes 786440 | tf_op jit(solution)/shard_map/ppermute | solution.py:262
  55.7 0.4 collective-permute-start.13
  56.1 6.8 %collective-permute-done.9 = bf16[256,512]{1,0:T(8,128)(2,1)S(1)} collective-permute-done((bf16[256,512]{1,0:T(8,128)(2,1)S(1)}, bf16[256,512]{1,0:T(8,128)(2,1)S(1)}, u32[]{:S(2)}, u32[]{:S(2)}) %collective-permute-start.9) | collective-permute-done | bytes 262176 | tf_op jit(solution)/shard_map/ppermute | solution.py:262
  62.9 0.1 add_convert_fusion.2
  63.0 1.9 %collective-permute-start.10 = (bf16[256,512]{1,0:T(8,128)(2,1)S(1)}, bf16[256,512]{1,0:T(8,128)(2,1)S(1)}, u32[]{:S(2)}, u32[]{:S(2)}) collective-permute-start(bf16[256,512]{1,0:T(8,128)(2,1)S(1)} %add_convert_fusion.2), channel_id=1, source_target_pairs={{16,0},{17,1},{20,4},{21,5},{24,8},{25,9},{28,12},{29,13},{32,16},... | collective-permute-start | bytes 786440 | tf_op jit(solution)/shard_map/ppermute | solution.py:262
  64.9 3.6 %collective-permute-done.11 = bf16[256,512]{1,0:T(8,128)(2,1)S(1)} collective-permute-done((bf16[256,512]{1,0:T(8,128)(2,1)S(1)}, bf16[256,512]{1,0:T(8,128)(2,1)S(1)}, u32[]{:S(2)}, u32[]{:S(2)}) %collective-permute-start.11) | collective-permute-done | bytes 262176 | tf_op jit(solution)/shard_map/ppermute | solution.py:262
  68.5 0.1 add_convert_fusion.1
  68.6 1.9 %collective-permute-start.12 = (bf16[256,512]{1,0:T(8,128)(2,1)S(1)}, bf16[256,512]{1,0:T(8,128)(2,1)S(1)}, u32[]{:S(2)}, u32[]{:S(2)}) collective-permute-start(bf16[256,512]{1,0:T(8,128)(2,1)S(1)} %add_convert_fusion.1), channel_id=1, source_target_pairs={{8,0},{9,1},{12,4},{13,5},{16,8},{17,9},{20,12},{21,13},{24,16},{2... | collective-permute-start | bytes 786440 | tf_op jit(solution)/shard_map/ppermute | solution.py:262
  70.5 0.1 collective-permute-start.8
  70.6 0.9 %collective-permute-done.13 = bf16[256,512]{1,0:T(8,128)(2,1)S(1)} collective-permute-done((bf16[256,512]{1,0:T(8,128)(2,1)}, bf16[256,512]{1,0:T(8,128)(2,1)S(1)}, u32[]{:S(2)}, u32[]{:S(2)}) %collective-permute-start.13) | collective-permute-done | bytes 262176 | tf_op jit(solution)/shard_map/ppermute | solution.py:262
  71.5 4.4 %collective-permute-done.10 = bf16[256,512]{1,0:T(8,128)(2,1)S(1)} collective-permute-done((bf16[256,512]{1,0:T(8,128)(2,1)S(1)}, bf16[256,512]{1,0:T(8,128)(2,1)S(1)}, u32[]{:S(2)}, u32[]{:S(2)}) %collective-permute-start.10) | collective-permute-done | bytes 262176 | tf_op jit(solution)/shard_map/ppermute | solution.py:262
  75.9 2.6 %collective-permute-done.12 = bf16[256,512]{1,0:T(8,128)(2,1)S(1)} collective-permute-done((bf16[256,512]{1,0:T(8,128)(2,1)S(1)}, bf16[256,512]{1,0:T(8,128)(2,1)S(1)}, u32[]{:S(2)}, u32[]{:S(2)}) %collective-permute-start.12) | collective-permute-done | bytes 262176 | tf_op jit(solution)/shard_map/ppermute | solution.py:262
  78.5 0.1 add_convert_fusion
  78.7 0.1 collective-permute-start.14
  78.8 0.0 collective-permute-done.8
  78.8 1.2 %maximum_select_fusion = bf16[128,4096]{1,0:T(8,128)(2,1)} fusion(bf16[128,2048]{1,0:T(8,128)(2,1)S(1)} %collective-permute-done.8, bf16[128,2048]{1,0:T(8,128)(2,1)S(1)} %get-tuple-element.21, pred[]{:T(512)S(6)} %eq.6), kind=kLoop, calls=%fused_computation | loop fusion | flops 4718592 | bytes 2097153 | tf_op jit(solution)/shard_map/jit(_where)/select_n | solution.py:269
  80.0 0.1 collective-permute-done.14.got_ref
  80.2 0.7 shard_map.78
  (3 shorter events, 0.1 us)
Async XLA Ops:
  0.6 10.3 %copy-start = (bf16[128,4096]{1,0:T(8,128)(2,1)S(1)}, bf16[128,4096]{1,0:T(8,128)(2,1)}, u32[]{:S(2)}) copy-start(bf16[128,4096]{1,0:T(8,128)(2,1)} %q_own_ref.1) | copy-start | bytes 3145732
  0.6 1.0 %copy-start.2 = (bf16[128,512]{1,0:T(8,128)(2,1)S(1)}, bf16[128,512]{1,0:T(8,128)(2,1)}, u32[]{:S(2)}) copy-start(bf16[128,512]{1,0:T(8,128)(2,1)} %keys_ref.1) | copy-start | bytes 393220
  1.6 0.9 %copy-start.3 = (bf16[128,512]{1,0:T(8,128)(2,1)S(1)}, bf16[128,512]{1,0:T(8,128)(2,1)}, u32[]{:S(2)}) copy-start(bf16[128,512]{1,0:T(8,128)(2,1)} %values_ref.1) | copy-start | bytes 393220
  2.6 2.5 %collective-permute-start.2 = (bf16[128,512]{1,0:T(8,128)(2,1)S(1)}, bf16[128,512]{1,0:T(8,128)(2,1)S(1)}, u32[]{:S(2)}, u32[]{:S(2)}) collective-permute-start(bf16[128,512]{1,0:T(8,128)(2,1)S(1)} %get-tuple-element.18), channel_id=1, source_target_pairs={{0,4},{1,5},{4,0},{5,1},{8,12},{9,13},{12,8},{13,9},{16,20},{17,21... | collective-permute-start | bytes 393224 | tf_op jit(solution)/shard_map/ppermute | solution.py:262
  4.6 30.6 %copy-start.1 = (bf16[128,4096]{1,0:T(8,128)(2,1)S(1)}, bf16[128,4096]{1,0:T(8,128)(2,1)}, u32[]{:S(2)}) copy-start(bf16[128,4096]{1,0:T(8,128)(2,1)} %g_own_ref.1) | copy-start | bytes 3145732
  4.6 30.6 %copy-start.4 = (s32[64]{0:T(128)S(1)}, s32[64]{0:T(128)}, u32[]{:S(2)}) copy-start(s32[64]{0:T(128)} %param.9) | copy-start | bytes 772
  4.6 21.7 %collective-permute-start.1 = (bf16[128,2048]{1,0:T(8,128)(2,1)}, bf16[128,2048]{1,0:T(8,128)(2,1)S(1)}, u32[]{:S(2)}, u32[]{:S(2)}) collective-permute-start(bf16[128,2048]{1,0:T(8,128)(2,1)} %constant_dynamic-slice_fusion.2), channel_id=1, source_target_pairs={{0,4},{1,5},{4,0},{5,1},{8,12},{9,13},{12,8},{13,9},{16,20},{17,21... | collective-permute-start | bytes 1572872 | tf_op jit(solution)/shard_map/ppermute | solution.py:262
  5.1 8.6 %collective-permute-start.6 = (bf16[256,512]{1,0:T(8,128)(2,1)S(1)}, bf16[256,512]{1,0:T(8,128)(2,1)S(1)}, u32[]{:S(2)}, u32[]{:S(2)}) collective-permute-start(bf16[256,512]{1,0:T(8,128)(2,1)S(1)} %maximum_select_fusion.1.pieces_4_), channel_id=1, source_target_pairs={{0,1},{1,0},{4,5},{5,4},{8,9},{9,8},{12,13},{13,12},{16,17},{17,16... | collective-permute-start | bytes 786440 | tf_op jit(solution)/shard_map/ppermute | solution.py:262
  6.8 16.4 %collective-permute-start.5 = (bf16[256,512]{1,0:T(8,128)(2,1)S(1)}, bf16[256,512]{1,0:T(8,128)(2,1)S(1)}, u32[]{:S(2)}, u32[]{:S(2)}) collective-permute-start(bf16[256,512]{1,0:T(8,128)(2,1)S(1)} %maximum_select_fusion.1.pieces_4_), channel_id=1, source_target_pairs={{0,8},{1,9},{4,12},{5,13},{8,16},{9,17},{12,20},{13,21},{16,24},{1... | collective-permute-start | bytes 786440 | tf_op jit(solution)/shard_map/ppermute | solution.py:262
  10.9 15.3 %collective-permute-start = (bf16[128,2048]{1,0:T(8,128)(2,1)S(1)}, bf16[128,2048]{1,0:T(8,128)(2,1)S(1)}, u32[]{:S(2)}, u32[]{:S(2)}) collective-permute-start(bf16[128,2048]{1,0:T(8,128)(2,1)S(1)} %constant_dynamic-slice_fusion.3), channel_id=1, source_target_pairs={{0,4},{1,5},{4,0},{5,1},{8,12},{9,13},{12,8},{13,9},{16,20},{17,21... | collective-permute-start | bytes 1572872 | tf_op jit(solution)/shard_map/ppermute | solution.py:262
  11.0 14.5 %collective-permute-start.3 = (bf16[256,512]{1,0:T(8,128)(2,1)S(1)}, bf16[256,512]{1,0:T(8,128)(2,1)S(1)}, u32[]{:S(2)}, u32[]{:S(2)}) collective-permute-start(bf16[256,512]{1,0:T(8,128)(2,1)S(1)} %maximum_select_fusion.1.pieces_4_), channel_id=1, source_target_pairs={{0,16},{1,17},{4,20},{5,21},{8,24},{9,25},{12,28},{13,29},{16,32},... | collective-permute-start | bytes 786440 | tf_op jit(solution)/shard_map/ppermute | solution.py:262
  23.2 8.1 %collective-permute-start.7 = (bf16[256,512]{1,0:T(8,128)(2,1)S(1)}, bf16[256,512]{1,0:T(8,128)(2,1)S(1)}, u32[]{:S(2)}, u32[]{:S(2)}) collective-permute-start(bf16[256,512]{1,0:T(8,128)(2,1)S(1)} %collective-permute-done.5.pieces_2_), channel_id=1, source_target_pairs={{0,1},{1,0},{4,5},{5,4},{8,9},{9,8},{12,13},{13,12},{16,17},{17,16... | collective-permute-start | bytes 786440 | tf_op jit(solution)/shard_map/ppermute | solution.py:262
  25.6 9.6 %collective-permute-start.4 = (bf16[256,512]{1,0:T(8,128)(2,1)S(1)}, bf16[256,512]{1,0:T(8,128)(2,1)S(1)}, u32[]{:S(2)}, u32[]{:S(2)}) collective-permute-start(bf16[256,512]{1,0:T(8,128)(2,1)S(1)} %collective-permute-done.3.pieces_0_), channel_id=1, source_target_pairs={{0,1},{1,0},{4,5},{5,4},{8,9},{9,8},{12,13},{13,12},{16,17},{17,16... | collective-permute-start | bytes 786440 | tf_op jit(solution)/shard_map/ppermute | solution.py:262
  53.7 9.2 %collective-permute-start.9 = (bf16[256,512]{1,0:T(8,128)(2,1)S(1)}, bf16[256,512]{1,0:T(8,128)(2,1)S(1)}, u32[]{:S(2)}, u32[]{:S(2)}) collective-permute-start(bf16[256,512]{1,0:T(8,128)(2,1)S(1)} %get-tuple-element.24), channel_id=1, source_target_pairs={{0,1},{1,0},{4,5},{5,4},{8,9},{9,8},{12,13},{13,12},{16,17},{17,16... | collective-permute-start | bytes 786440 | tf_op jit(solution)/shard_map/ppermute | solution.py:262
  54.1 14.4 %collective-permute-start.11 = (bf16[256,512]{1,0:T(8,128)(2,1)S(1)}, bf16[256,512]{1,0:T(8,128)(2,1)S(1)}, u32[]{:S(2)}, u32[]{:S(2)}) collective-permute-start(bf16[256,512]{1,0:T(8,128)(2,1)S(1)} %get-tuple-element.26), channel_id=1, source_target_pairs={{0,1},{1,0},{4,5},{5,4},{8,9},{9,8},{12,13},{13,12},{16,17},{17,16... | collective-permute-start | bytes 786440 | tf_op jit(solution)/shard_map/ppermute | solution.py:262
  55.7 15.8 %collective-permute-start.13 = (bf16[256,512]{1,0:T(8,128)(2,1)}, bf16[256,512]{1,0:T(8,128)(2,1)S(1)}, u32[]{:S(2)}, u32[]{:S(2)}) collective-permute-start(bf16[256,512]{1,0:T(8,128)(2,1)} %get-tuple-element.28), channel_id=1, source_target_pairs={{0,1},{1,0},{4,5},{5,4},{8,9},{9,8},{12,13},{13,12},{16,17},{17,16... | collective-permute-start | bytes 786440 | tf_op jit(solution)/shard_map/ppermute | solution.py:262
  63.0 12.9 %collective-permute-start.10 = (bf16[256,512]{1,0:T(8,128)(2,1)S(1)}, bf16[256,512]{1,0:T(8,128)(2,1)S(1)}, u32[]{:S(2)}, u32[]{:S(2)}) collective-permute-start(bf16[256,512]{1,0:T(8,128)(2,1)S(1)} %add_convert_fusion.2), channel_id=1, source_target_pairs={{16,0},{17,1},{20,4},{21,5},{24,8},{25,9},{28,12},{29,13},{32,16},... | collective-permute-start | bytes 786440 | tf_op jit(solution)/shard_map/ppermute | solution.py:262
  68.6 10.0 %collective-permute-start.12 = (bf16[256,512]{1,0:T(8,128)(2,1)S(1)}, bf16[256,512]{1,0:T(8,128)(2,1)S(1)}, u32[]{:S(2)}, u32[]{:S(2)}) collective-permute-start(bf16[256,512]{1,0:T(8,128)(2,1)S(1)} %add_convert_fusion.1), channel_id=1, source_target_pairs={{8,0},{9,1},{12,4},{13,5},{16,8},{17,9},{20,12},{21,13},{24,16},{2... | collective-permute-start | bytes 786440 | tf_op jit(solution)/shard_map/ppermute | solution.py:262
  70.5 8.3 %collective-permute-start.8 = (bf16[128,2048]{1,0:T(8,128)(2,1)}, bf16[128,2048]{1,0:T(8,128)(2,1)S(1)}, u32[]{:S(2)}, u32[]{:S(2)}) collective-permute-start(bf16[128,2048]{1,0:T(8,128)(2,1)} %get-tuple-element.22), channel_id=1, source_target_pairs={{0,4},{1,5},{4,0},{5,1},{8,12},{9,13},{12,8},{13,9},{16,20},{17,21... | collective-permute-start | bytes 1572872 | tf_op jit(solution)/shard_map/ppermute | solution.py:262
  78.7 1.4 %collective-permute-start.14 = (bf16[128,512]{1,0:T(8,128)(2,1)S(1)}, bf16[128,512]{1,0:T(8,128)(2,1)S(1)}, u32[]{:S(2)}, u32[]{:S(2)}) collective-permute-start(bf16[128,512]{1,0:T(8,128)(2,1)S(1)} %get-tuple-element.31), channel_id=1, source_target_pairs={{0,4},{1,5},{4,0},{5,1},{8,12},{9,13},{12,8},{13,9},{16,20},{17,21... | collective-permute-start | bytes 393224 | tf_op jit(solution)/shard_map/ppermute | solution.py:262

commit v4 on v3

--- a/solution.py
+++ b/solution.py
@@ -275,7 +275,11 @@
 
     chunk = jax.ShapeDtypeStruct(keys.shape, jnp.bfloat16)
     small = pltpu.CompilerParams(vmem_limit_bytes=4 * 2**20)
-    mine, given = pl.pallas_call(split_kernel, out_shape=[chunk, chunk], compiler_params=small)(keys, values)
+    mine, given = pl.pallas_call(
+        split_kernel,
+        out_shape=[chunk, chunk],
+        compiler_params=pltpu.CompilerParams(vmem_limit_bytes=56 * 2**20),
+    )(keys, values)
     own = in_order(mine, sent(given, swap_core), 0)
     far, near, beside = sent(own, ahead(n_ctx, 2)), sent(own, ahead(n_ctx, 1)), sent(own, swap_part)
     near, beside = lax.optimization_barrier((near, beside))

time: 81.9 us -> 80.9 us (0.988)
  local copies, waits for them, and re-layouts: 3.86 us -> 1.2 us
  Pallas kernels: 19.2 us -> 21 us
    unnamed x10 -> x8, local copies, waits for them, and re-layouts: 1.9 us -> 0.02 us
    pallas_call x1, Pallas kernels: 0.05 us -> 1.8 us  [body(): pl.pallas_call(split_kernel, out_shape=[chunk, chunk], compiler_params=pl...]
  transfers between devices with their start and end apart: 15 -> 15, of which waited for: 10 -> 10; matrix products, arithmetic and copies ran while one was open for 4% -> 3% of each run, Pallas kernels for 0% -> 0%
where the time goes in v4:
time: 80.9 us; the launch traced here: 80 us
  waiting for transfers between devices  38.7 us (48%)
  Pallas kernels  21 us (26%)
  starting transfers between devices  16.7 us (21%)
  other arithmetic  1.54 us (2%)
  local copies, waits for them, and re-layouts  1.2 us (1%)
    ppermute x15, waiting for transfers between devices, sent(): return lax.ppermute(value, AXES, plan)  38.7 us
    pallas_call x1, Pallas kernels, attention(): pl.pallas_call(kernel, grid=(kv_heads,), in_specs=[pl.BlockSpec(lengths.s...  18.4 us
    ppermute x15, starting transfers between devices, sent(): return lax.ppermute(value, AXES, plan)  16.7 us
    pallas_call x1, Pallas kernels, body(): pl.pallas_call(split_kernel, out_shape=[chunk, chunk], compiler_params=pl...  1.8 us
  transfers between devices with their start and end apart: 15, of which 10 were waited for; matrix products, arithmetic and copies ran while one was open for 3% of the time, Pallas kernels for 0%

profile of v4, /device:TPU:230, one launch (start us, length us, event | category | flops | bytes accessed | tf_op | source)
XLA Modules:
  0.0 80.0 jit_solution(13255757307595495471)
XLA Ops:
  0.6 0.0 copy-start
  0.6 1.8 %shard_map.76 = (bf16[128,512]{1,0:T(8,128)(2,1)}, bf16[128,512]{1,0:T(8,128)(2,1)}) custom-call(bf16[128,512]{1,0:T(8,128)(2,1)} %keys_ref.1, bf16[128,512]{1,0:T(8,128)(2,1)} %values_ref.1), custom_call_target="tpu_custom_call" | custom-call | tf_op jit(solution)/shard_map/pallas_call | solution.py:278
  2.4 0.0 copy-start.3
  2.4 0.0 collective-permute-start.2
  2.4 1.1 %constant_dynamic-slice_fusion.2 = bf16[128,2048]{1,0:T(8,128)(2,1)S(1)} fusion(bf16[128,4096]{1,0:T(8,128)(2,1)} %g_own_ref.1, s32[]{:T(128)S(6)} %select_n.35), kind=kLoop, calls=%fused_computation.7 | loop fusion | bytes 1048580 | tf_op jit(solution)/shard_map/dynamic_slice | solution.py:266
  3.6 0.0 copy-start.1
  3.6 0.0 copy-start.2
  3.6 0.6 collective-permute-start.1
  4.1 0.0 collective-permute-done.2
  4.1 0.0 copy-done.3
  4.1 0.1 maximum_select_fusion.1.pieces_4_
  4.2 1.7 %collective-permute-start.6 = (bf16[256,512]{1,0:T(8,128)(2,1)S(1)}, bf16[256,512]{1,0:T(8,128)(2,1)S(1)}, u32[]{:S(2)}, u32[]{:S(2)}) collective-permute-start(bf16[256,512]{1,0:T(8,128)(2,1)S(1)} %maximum_select_fusion.1.pieces_4_), channel_id=1, source_target_pairs={{0,1},{1,0},{4,5},{5,4},{8,9},{9,8},{12,13},{13,12},{16,17},{17,16... | collective-permute-start | bytes 786440 | tf_op jit(solution)/shard_map/ppermute | solution.py:262
  5.9 4.1 %collective-permute-start.5 = (bf16[256,512]{1,0:T(8,128)(2,1)S(1)}, bf16[256,512]{1,0:T(8,128)(2,1)S(1)}, u32[]{:S(2)}, u32[]{:S(2)}) collective-permute-start(bf16[256,512]{1,0:T(8,128)(2,1)S(1)} %maximum_select_fusion.1.pieces_4_), channel_id=1, source_target_pairs={{0,8},{1,9},{4,12},{5,13},{8,16},{9,17},{12,20},{13,21},{16,24},{1... | collective-permute-start | bytes 786440 | tf_op jit(solution)/shard_map/ppermute | solution.py:262
  10.0 0.0 copy-done
  10.0 0.1 collective-permute-start
  10.1 2.7 %collective-permute-start.3 = (bf16[256,512]{1,0:T(8,128)(2,1)S(1)}, bf16[256,512]{1,0:T(8,128)(2,1)S(1)}, u32[]{:S(2)}, u32[]{:S(2)}) collective-permute-start(bf16[256,512]{1,0:T(8,128)(2,1)S(1)} %maximum_select_fusion.1.pieces_4_), channel_id=1, source_target_pairs={{0,16},{1,17},{4,20},{5,21},{8,24},{9,25},{12,28},{13,29},{16,32},... | collective-permute-start | bytes 786440 | tf_op jit(solution)/shard_map/ppermute | solution.py:262
  12.8 0.0 collective-permute-done.6.pieces_5_
  12.8 9.4 %collective-permute-done.5.pieces_2_ = bf16[256,512]{1,0:T(8,128)(2,1)S(1)} collective-permute-done((bf16[256,512]{1,0:T(8,128)(2,1)S(1)}, bf16[256,512]{1,0:T(8,128)(2,1)S(1)}, u32[]{:S(2)}, u32[]{:S(2)}) %collective-permute-start.5) | collective-permute-done | bytes 262176 | tf_op jit(solution)/shard_map/ppermute | solution.py:262
  22.3 0.4 collective-permute-start.7
  22.7 1.9 %collective-permute-done.3.pieces_0_ = bf16[256,512]{1,0:T(8,128)(2,1)S(1)} collective-permute-done((bf16[256,512]{1,0:T(8,128)(2,1)S(1)}, bf16[256,512]{1,0:T(8,128)(2,1)S(1)}, u32[]{:S(2)}, u32[]{:S(2)}) %collective-permute-start.3) | collective-permute-done | bytes 262176 | tf_op jit(solution)/shard_map/ppermute | solution.py:262
  24.6 0.7 collective-permute-start.4
  25.3 0.0 collective-permute-done.1.g_got_ref
  25.3 0.0 collective-permute-done.q_got_ref
  25.3 5.0 %collective-permute-done.7.pieces_3_ = bf16[256,512]{1,0:T(8,128)(2,1)S(1)} collective-permute-done((bf16[256,512]{1,0:T(8,128)(2,1)S(1)}, bf16[256,512]{1,0:T(8,128)(2,1)S(1)}, u32[]{:S(2)}, u32[]{:S(2)}) %collective-permute-start.7) | collective-permute-done | bytes 262176 | tf_op jit(solution)/shard_map/ppermute | solution.py:262
  30.4 3.9 %collective-permute-done.4.pieces_1_ = bf16[256,512]{1,0:T(8,128)(2,1)S(1)} collective-permute-done((bf16[256,512]{1,0:T(8,128)(2,1)S(1)}, bf16[256,512]{1,0:T(8,128)(2,1)S(1)}, u32[]{:S(2)}, u32[]{:S(2)}) %collective-permute-start.4) | collective-permute-done | bytes 262176 | tf_op jit(solution)/shard_map/ppermute | solution.py:262
  34.3 0.0 copy-done.1
  34.3 0.0 copy-done.2
  34.3 18.4 %shard_map.77 = (bf16[128,2048]{1,0:T(8,128)(2,1)S(1)}, bf16[128,2048]{1,0:T(8,128)(2,1)}, bf16[256,512]{1,0:T(8,128)(2,1)S(1)}, bf16[256,512]{1,0:T(8,128)(2,1)...) custom-call(s32[1,64]{1,0:T(1,128)S(1)} %bitcast.1, ...), custom_call_target="tpu_custom_call" | custom-call | tf_op jit(solution)/shard_map/pallas_call | solution.py:226
  52.7 0.4 collective-permute-start.9
  53.2 1.6 %collective-permute-start.11 = (bf16[256,512]{1,0:T(8,128)(2,1)S(1)}, bf16[256,512]{1,0:T(8,128)(2,1)S(1)}, u32[]{:S(2)}, u32[]{:S(2)}) collective-permute-start(bf16[256,512]{1,0:T(8,128)(2,1)S(1)} %get-tuple-element.26), channel_id=1, source_target_pairs={{0,1},{1,0},{4,5},{5,4},{8,9},{9,8},{12,13},{13,12},{16,17},{17,16... | collective-permute-start | bytes 786440 | tf_op jit(solution)/shard_map/ppermute | solution.py:262
  54.8 0.4 collective-permute-start.13
  55.2 6.8 %collective-permute-done.9 = bf16[256,512]{1,0:T(8,128)(2,1)S(1)} collective-permute-done((bf16[256,512]{1,0:T(8,128)(2,1)S(1)}, bf16[256,512]{1,0:T(8,128)(2,1)S(1)}, u32[]{:S(2)}, u32[]{:S(2)}) %collective-permute-start.9) | collective-permute-done | bytes 262176 | tf_op jit(solution)/shard_map/ppermute | solution.py:262
  62.0 0.1 add_convert_fusion.2
  62.1 1.9 %collective-permute-start.10 = (bf16[256,512]{1,0:T(8,128)(2,1)S(1)}, bf16[256,512]{1,0:T(8,128)(2,1)S(1)}, u32[]{:S(2)}, u32[]{:S(2)}) collective-permute-start(bf16[256,512]{1,0:T(8,128)(2,1)S(1)} %add_convert_fusion.2), channel_id=1, source_target_pairs={{16,0},{17,1},{20,4},{21,5},{24,8},{25,9},{28,12},{29,13},{32,16},... | collective-permute-start | bytes 786440 | tf_op jit(solution)/shard_map/ppermute | solution.py:262
  64.0 3.6 %collective-permute-done.11 = bf16[256,512]{1,0:T(8,128)(2,1)S(1)} collective-permute-done((bf16[256,512]{1,0:T(8,128)(2,1)S(1)}, bf16[256,512]{1,0:T(8,128)(2,1)S(1)}, u32[]{:S(2)}, u32[]{:S(2)}) %collective-permute-start.11) | collective-permute-done | bytes 262176 | tf_op jit(solution)/shard_map/ppermute | solution.py:262
  67.6 0.1 add_convert_fusion.1
  67.7 1.9 %collective-permute-start.12 = (bf16[256,512]{1,0:T(8,128)(2,1)S(1)}, bf16[256,512]{1,0:T(8,128)(2,1)S(1)}, u32[]{:S(2)}, u32[]{:S(2)}) collective-permute-start(bf16[256,512]{1,0:T(8,128)(2,1)S(1)} %add_convert_fusion.1), channel_id=1, source_target_pairs={{8,0},{9,1},{12,4},{13,5},{16,8},{17,9},{20,12},{21,13},{24,16},{2... | collective-permute-start | bytes 786440 | tf_op jit(solution)/shard_map/ppermute | solution.py:262
  69.6 0.1 collective-permute-start.8
  69.7 0.9 %collective-permute-done.13 = bf16[256,512]{1,0:T(8,128)(2,1)S(1)} collective-permute-done((bf16[256,512]{1,0:T(8,128)(2,1)}, bf16[256,512]{1,0:T(8,128)(2,1)S(1)}, u32[]{:S(2)}, u32[]{:S(2)}) %collective-permute-start.13) | collective-permute-done | bytes 262176 | tf_op jit(solution)/shard_map/ppermute | solution.py:262
  70.6 4.4 %collective-permute-done.10 = bf16[256,512]{1,0:T(8,128)(2,1)S(1)} collective-permute-done((bf16[256,512]{1,0:T(8,128)(2,1)S(1)}, bf16[256,512]{1,0:T(8,128)(2,1)S(1)}, u32[]{:S(2)}, u32[]{:S(2)}) %collective-permute-start.10) | collective-permute-done | bytes 262176 | tf_op jit(solution)/shard_map/ppermute | solution.py:262
  75.0 2.6 %collective-permute-done.12 = bf16[256,512]{1,0:T(8,128)(2,1)S(1)} collective-permute-done((bf16[256,512]{1,0:T(8,128)(2,1)S(1)}, bf16[256,512]{1,0:T(8,128)(2,1)S(1)}, u32[]{:S(2)}, u32[]{:S(2)}) %collective-permute-start.12) | collective-permute-done | bytes 262176 | tf_op jit(solution)/shard_map/ppermute | solution.py:262
  77.6 0.1 add_convert_fusion
  77.8 0.1 collective-permute-start.14
  77.9 0.0 collective-permute-done.8
  77.9 1.2 %maximum_select_fusion = bf16[128,4096]{1,0:T(8,128)(2,1)} fusion(bf16[128,2048]{1,0:T(8,128)(2,1)S(1)} %collective-permute-done.8, bf16[128,2048]{1,0:T(8,128)(2,1)S(1)} %get-tuple-element.21, pred[]{:T(512)S(6)} %eq.6), kind=kLoop, calls=%fused_computation | loop fusion | flops 4718592 | bytes 2097153 | tf_op jit(solution)/shard_map/jit(_where)/select_n | solution.py:269
  79.1 0.1 collective-permute-done.14.got_ref
  79.2 0.7 shard_map.78
  (2 shorter events, 0.1 us)
Async XLA Ops:
  0.6 9.3 %copy-start = (bf16[128,4096]{1,0:T(8,128)(2,1)S(1)}, bf16[128,4096]{1,0:T(8,128)(2,1)}, u32[]{:S(2)}) copy-start(bf16[128,4096]{1,0:T(8,128)(2,1)} %q_own_ref.1) | copy-start | bytes 3145732
  2.4 1.7 %copy-start.3 = (bf16[128,512]{1,0:T(8,128)(2,1)S(1)}, bf16[128,512]{1,0:T(8,128)(2,1)}, u32[]{:S(2)}) copy-start(bf16[128,512]{1,0:T(8,128)(2,1)} %get-tuple-element.17) | copy-start | bytes 393220
  2.4 1.7 %collective-permute-start.2 = (bf16[128,512]{1,0:T(8,128)(2,1)}, bf16[128,512]{1,0:T(8,128)(2,1)S(1)}, u32[]{:S(2)}, u32[]{:S(2)}) collective-permute-start(bf16[128,512]{1,0:T(8,128)(2,1)} %get-tuple-element.18), channel_id=1, source_target_pairs={{0,4},{1,5},{4,0},{5,1},{8,12},{9,13},{12,8},{13,9},{16,20},{17,21... | collective-permute-start | bytes 393224 | tf_op jit(solution)/shard_map/ppermute | solution.py:262
  3.6 30.7 %copy-start.1 = (bf16[128,4096]{1,0:T(8,128)(2,1)S(1)}, bf16[128,4096]{1,0:T(8,128)(2,1)}, u32[]{:S(2)}) copy-start(bf16[128,4096]{1,0:T(8,128)(2,1)} %g_own_ref.1) | copy-start | bytes 3145732
  3.6 30.7 %copy-start.2 = (s32[64]{0:T(128)S(1)}, s32[64]{0:T(128)}, u32[]{:S(2)}) copy-start(s32[64]{0:T(128)} %param.9) | copy-start | bytes 772
  3.6 21.7 %collective-permute-start.1 = (bf16[128,2048]{1,0:T(8,128)(2,1)S(1)}, bf16[128,2048]{1,0:T(8,128)(2,1)S(1)}, u32[]{:S(2)}, u32[]{:S(2)}) collective-permute-start(bf16[128,2048]{1,0:T(8,128)(2,1)S(1)} %constant_dynamic-slice_fusion.2), channel_id=1, source_target_pairs={{0,4},{1,5},{4,0},{5,1},{8,12},{9,13},{12,8},{13,9},{16,20},{17,21... | collective-permute-start | bytes 1572872 | tf_op jit(solution)/shard_map/ppermute | solution.py:262
  4.2 8.6 %collective-permute-start.6 = (bf16[256,512]{1,0:T(8,128)(2,1)S(1)}, bf16[256,512]{1,0:T(8,128)(2,1)S(1)}, u32[]{:S(2)}, u32[]{:S(2)}) collective-permute-start(bf16[256,512]{1,0:T(8,128)(2,1)S(1)} %maximum_select_fusion.1.pieces_4_), channel_id=1, source_target_pairs={{0,1},{1,0},{4,5},{5,4},{8,9},{9,8},{12,13},{13,12},{16,17},{17,16... | collective-permute-start | bytes 786440 | tf_op jit(solution)/shard_map/ppermute | solution.py:262
  5.9 16.4 %collective-permute-start.5 = (bf16[256,512]{1,0:T(8,128)(2,1)S(1)}, bf16[256,512]{1,0:T(8,128)(2,1)S(1)}, u32[]{:S(2)}, u32[]{:S(2)}) collective-permute-start(bf16[256,512]{1,0:T(8,128)(2,1)S(1)} %maximum_select_fusion.1.pieces_4_), channel_id=1, source_target_pairs={{0,8},{1,9},{4,12},{5,13},{8,16},{9,17},{12,20},{13,21},{16,24},{1... | collective-permute-start | bytes 786440 | tf_op jit(solution)/shard_map/ppermute | solution.py:262
  10.0 15.3 %collective-permute-start = (bf16[128,2048]{1,0:T(8,128)(2,1)S(1)}, bf16[128,2048]{1,0:T(8,128)(2,1)S(1)}, u32[]{:S(2)}, u32[]{:S(2)}) collective-permute-start(bf16[128,2048]{1,0:T(8,128)(2,1)S(1)} %constant_dynamic-slice_fusion.3), channel_id=1, source_target_pairs={{0,4},{1,5},{4,0},{5,1},{8,12},{9,13},{12,8},{13,9},{16,20},{17,21... | collective-permute-start | bytes 1572872 | tf_op jit(solution)/shard_map/ppermute | solution.py:262
  10.1 14.5 %collective-permute-start.3 = (bf16[256,512]{1,0:T(8,128)(2,1)S(1)}, bf16[256,512]{1,0:T(8,128)(2,1)S(1)}, u32[]{:S(2)}, u32[]{:S(2)}) collective-permute-start(bf16[256,512]{1,0:T(8,128)(2,1)S(1)} %maximum_select_fusion.1.pieces_4_), channel_id=1, source_target_pairs={{0,16},{1,17},{4,20},{5,21},{8,24},{9,25},{12,28},{13,29},{16,32},... | collective-permute-start | bytes 786440 | tf_op jit(solution)/shard_map/ppermute | solution.py:262
  22.3 8.1 %collective-permute-start.7 = (bf16[256,512]{1,0:T(8,128)(2,1)S(1)}, bf16[256,512]{1,0:T(8,128)(2,1)S(1)}, u32[]{:S(2)}, u32[]{:S(2)}) collective-permute-start(bf16[256,512]{1,0:T(8,128)(2,1)S(1)} %collective-permute-done.5.pieces_2_), channel_id=1, source_target_pairs={{0,1},{1,0},{4,5},{5,4},{8,9},{9,8},{12,13},{13,12},{16,17},{17,16... | collective-permute-start | bytes 786440 | tf_op jit(solution)/shard_map/ppermute | solution.py:262
  24.6 9.6 %collective-permute-start.4 = (bf16[256,512]{1,0:T(8,128)(2,1)S(1)}, bf16[256,512]{1,0:T(8,128)(2,1)S(1)}, u32[]{:S(2)}, u32[]{:S(2)}) collective-permute-start(bf16[256,512]{1,0:T(8,128)(2,1)S(1)} %collective-permute-done.3.pieces_0_), channel_id=1, source_target_pairs={{0,1},{1,0},{4,5},{5,4},{8,9},{9,8},{12,13},{13,12},{16,17},{17,16... | collective-permute-start | bytes 786440 | tf_op jit(solution)/shard_map/ppermute | solution.py:262
  52.7 9.2 %collective-permute-start.9 = (bf16[256,512]{1,0:T(8,128)(2,1)S(1)}, bf16[256,512]{1,0:T(8,128)(2,1)S(1)}, u32[]{:S(2)}, u32[]{:S(2)}) collective-permute-start(bf16[256,512]{1,0:T(8,128)(2,1)S(1)} %get-tuple-element.24), channel_id=1, source_target_pairs={{0,1},{1,0},{4,5},{5,4},{8,9},{9,8},{12,13},{13,12},{16,17},{17,16... | collective-permute-start | bytes 786440 | tf_op jit(solution)/shard_map/ppermute | solution.py:262
  53.2 14.4 %collective-permute-start.11 = (bf16[256,512]{1,0:T(8,128)(2,1)S(1)}, bf16[256,512]{1,0:T(8,128)(2,1)S(1)}, u32[]{:S(2)}, u32[]{:S(2)}) collective-permute-start(bf16[256,512]{1,0:T(8,128)(2,1)S(1)} %get-tuple-element.26), channel_id=1, source_target_pairs={{0,1},{1,0},{4,5},{5,4},{8,9},{9,8},{12,13},{13,12},{16,17},{17,16... | collective-permute-start | bytes 786440 | tf_op jit(solution)/shard_map/ppermute | solution.py:262
  54.8 15.8 %collective-permute-start.13 = (bf16[256,512]{1,0:T(8,128)(2,1)}, bf16[256,512]{1,0:T(8,128)(2,1)S(1)}, u32[]{:S(2)}, u32[]{:S(2)}) collective-permute-start(bf16[256,512]{1,0:T(8,128)(2,1)} %get-tuple-element.28), channel_id=1, source_target_pairs={{0,1},{1,0},{4,5},{5,4},{8,9},{9,8},{12,13},{13,12},{16,17},{17,16... | collective-permute-start | bytes 786440 | tf_op jit(solution)/shard_map/ppermute | solution.py:262
  62.1 12.9 %collective-permute-start.10 = (bf16[256,512]{1,0:T(8,128)(2,1)S(1)}, bf16[256,512]{1,0:T(8,128)(2,1)S(1)}, u32[]{:S(2)}, u32[]{:S(2)}) collective-permute-start(bf16[256,512]{1,0:T(8,128)(2,1)S(1)} %add_convert_fusion.2), channel_id=1, source_target_pairs={{16,0},{17,1},{20,4},{21,5},{24,8},{25,9},{28,12},{29,13},{32,16},... | collective-permute-start | bytes 786440 | tf_op jit(solution)/shard_map/ppermute | solution.py:262
  67.7 10.0 %collective-permute-start.12 = (bf16[256,512]{1,0:T(8,128)(2,1)S(1)}, bf16[256,512]{1,0:T(8,128)(2,1)S(1)}, u32[]{:S(2)}, u32[]{:S(2)}) collective-permute-start(bf16[256,512]{1,0:T(8,128)(2,1)S(1)} %add_convert_fusion.1), channel_id=1, source_target_pairs={{8,0},{9,1},{12,4},{13,5},{16,8},{17,9},{20,12},{21,13},{24,16},{2... | collective-permute-start | bytes 786440 | tf_op jit(solution)/shard_map/ppermute | solution.py:262
  69.6 8.3 %collective-permute-start.8 = (bf16[128,2048]{1,0:T(8,128)(2,1)}, bf16[128,2048]{1,0:T(8,128)(2,1)S(1)}, u32[]{:S(2)}, u32[]{:S(2)}) collective-permute-start(bf16[128,2048]{1,0:T(8,128)(2,1)} %get-tuple-element.22), channel_id=1, source_target_pairs={{0,4},{1,5},{4,0},{5,1},{8,12},{9,13},{12,8},{13,9},{16,20},{17,21... | collective-permute-start | bytes 1572872 | tf_op jit(solution)/shard_map/ppermute | solution.py:262
  77.8 1.4 %collective-permute-start.14 = (bf16[128,512]{1,0:T(8,128)(2,1)S(1)}, bf16[128,512]{1,0:T(8,128)(2,1)S(1)}, u32[]{:S(2)}, u32[]{:S(2)}) collective-permute-start(bf16[128,512]{1,0:T(8,128)(2,1)S(1)} %get-tuple-element.31), channel_id=1, source_target_pairs={{0,4},{1,5},{4,0},{5,1},{8,12},{9,13},{12,8},{13,9},{16,20},{17,21... | collective-permute-start | bytes 393224 | tf_op jit(solution)/shard_map/ppermute | solution.py:262
